TPU v7x, 128 devices: a whole 4x4x4 slice. The times are simulated.
128 devices in a mesh: ctx: 32 (over z, x, core), head: 4 (over y).
Axes of the slice: x: 4, y: 4, z: 4, core: 2. Of those that a mesh axis runs over, the one named last changes fastest.
Arguments:
- queries: bfloat16 [16384, 7168], P(('ctx', 'head')), may hold values from -6 to 6
- keys_in: bfloat16 [16384, 7168], P(('ctx', 'head')), may hold values from -6 to 6
- values_in: bfloat16 [16384, 7168], P(('ctx', 'head')), may hold values from -6 to 6
- ssm_input: bfloat16 [16384, 7168], P('ctx', 'head'), may hold values from -6 to 6
- step_size: float32 [16384, 112], P('ctx', 'head'), may hold values from 0.5 to 2
- in_proj_b: bfloat16 [16384, 128], P('ctx'), may hold values from -6 to 6
- out_proj_c: bfloat16 [16384, 128], P('ctx'), may hold values from -0.75 to 0.75
- decay_rate: float32 [112], P('head'), may hold values from 0.0001 to 0.05
- skip_gain: float32 [112], P('head'), may hold values from 0.5 to 1.5
- doc_lengths: int32 [64], replicated, may hold values from 1 to 1536, 16384 in all
Outputs:
- attn_out: bfloat16 [16384, 7168], P(('ctx', 'head'))
- ssm_out: bfloat16 [16384, 7168], P('ctx', 'head')
Inputs may be any that keep to these rules, and one draw needn't show every extreme that they name: `doc_lengths`: the lengths sum to 16384; the longest is exactly 1536.
All inputs are finite; a program needn't handle non-finite values.
Results may differ from a plain program's by a relative error of at most 0.003.
Values may be sent and summed in bfloat16 or wider, within the bound.
No kernel may reach another device: no remote copies, remote signals or barrier semaphores. Data moves between devices by JAX's collectives and lax.ppermute only.
A program may use at most 256 MiB of HBM per device.

v0:
```python
import jax
import jax.numpy as jnp
from jax import lax
from jax.sharding import PartitionSpec as P

ATT_HD = 224
M_GROUPS = 2
SCAN_LEN = 256


def shifted(block, axis, distance):
    devices = range(lax.axis_size(axis))
    route = [(i - distance, i) for i in devices if i - distance in devices]
    return lax.ppermute(block, axis, route)


def entering(part, axis, combine, identity):
    place = lax.axis_index(axis)
    gathered = jax.tree.map(lambda a: lax.all_gather(a, axis), part)
    state = jax.tree.map(lambda a, e: jnp.zeros_like(a) + jnp.asarray(e, a.dtype), part, identity)

    def one(turn, state):
        return combine(
            state, jax.tree.map(lambda a: lax.dynamic_index_in_dim(a, turn, 0, False), gathered)
        )

    return lax.fori_loop(0, place, one, state)


def doc_of(positions, doc_lengths):
    ends = jnp.cumsum(doc_lengths)
    count = jnp.sum((ends[None, :] <= positions[:, None]).astype(jnp.int32), axis=1)
    return jnp.where(positions >= 0, count, -1)


def ssd_local(xs, step, b_in, c_in, rate, docs, doc_before, span):
    length = xs.shape[0]
    heads = step.shape[1]
    width = xs.shape[1] // heads
    count = length // span
    decay = -rate[None, :] * step
    cumul = jnp.cumsum(decay, axis=0)
    base = jnp.concatenate(
        [jnp.zeros((1, heads), cumul.dtype), cumul[span - 1 :: span][:-1]], axis=0
    )
    doc_prev = jnp.concatenate([jnp.reshape(doc_before, (1,)), docs[span - 1 :: span][:-1]], axis=0)
    x_blocks = jnp.reshape(xs.astype(cumul.dtype), (count, span, heads, width))
    hp = lax.Precision.HIGHEST
    order = jnp.arange(span)
    lower = order[None, :] <= order[:, None]

    def advance(state, pieces):
        x_c, dt_c, b_c, c_c, cum_c, doc_c, base_c, prev_c = pieces
        rel = cum_c - base_c[None, :]
        gram = jnp.dot(c_c, b_c.T, preferred_element_type=jnp.float32)
        b_wide = b_c.astype(cumul.dtype)
        c_wide = c_c.astype(cumul.dtype)
        rel_h = rel.T
        diff = rel_h[:, :, None] - rel_h[:, None, :]
        valid = jnp.logical_and(lower, doc_c[:, None] == doc_c[None, :])
        decays = jnp.where(valid[None], jnp.exp(jnp.where(valid[None], diff, 0.0)), 0.0)
        mixing = decays * gram[None] * dt_c.T[:, None, :]
        out = jnp.einsum("hts,shp->thp", mixing, x_c, precision=hp)
        carried = (doc_c == prev_c).astype(cumul.dtype)
        entry = jnp.exp(rel) * carried[:, None]
        out = out + entry[:, :, None] * jnp.einsum("tn,hnp->thp", c_wide, state, precision=hp)
        last = rel[-1]
        same = (doc_c == doc_c[-1]).astype(cumul.dtype)
        factor = jnp.exp(last[None, :] - rel) * same[:, None] * dt_c
        fresh = jnp.einsum("sh,sn,shp->hnp", factor, b_wide, x_c, precision=hp)
        link = jnp.exp(last) * (doc_c[-1] == prev_c).astype(cumul.dtype)
        return (link[:, None, None] * state + fresh, out)

    start = jnp.zeros((heads, b_in.shape[1], width), cumul.dtype)
    pieces = (
        x_blocks,
        jnp.reshape(step, (count, span, heads)),
        jnp.reshape(b_in, (count, span, -1)),
        jnp.reshape(c_in, (count, span, -1)),
        jnp.reshape(cumul, (count, span, heads)),
        jnp.reshape(docs, (count, span)),
        base,
        doc_prev,
    )
    final, outs = lax.scan(advance, start, pieces)
    link_all = jnp.exp(cumul[-1]) * (docs[-1] == doc_before).astype(cumul.dtype)
    return (jnp.reshape(outs, (length, heads * width)), final, link_all, cumul)


def combine_states(earlier, later):
    return (earlier[0] * later[0], later[0][:, None, None] * earlier[1] + later[1])


def attend(q_rows, k_rows, v_rows, qpos, kpos, qdoc, kdoc, heads):
    rows = q_rows.shape[0]
    extent = k_rows.shape[0]
    size = q_rows.shape[1] // heads
    q3 = jnp.reshape(q_rows, (rows, heads, size))
    k3 = jnp.reshape(k_rows, (extent, heads, size))
    v3 = jnp.reshape(v_rows, (extent, heads, size))
    scores = jnp.einsum("qhd,khd->hqk", q3, k3, preferred_element_type=jnp.float32) * (
        1.0 / size**0.5
    )
    kept = jnp.logical_and(kdoc[None, :] == qdoc[:, None], kpos[None, :] <= qpos[:, None])
    scores = jnp.where(kept[None], scores, -1e30)
    top = jnp.max(scores, axis=2, keepdims=True)
    weights = jnp.where(kept[None], jnp.exp(scores - top), 0.0)
    total = jnp.sum(weights, axis=2)
    weights_b = weights.astype(jnp.bfloat16)
    mixed = (
        jnp.einsum("hqk,khd->qhd", weights_b, v3, preferred_element_type=jnp.float32)
        / total.T[:, :, None]
    )
    return jnp.reshape(mixed, (rows, heads * size)).astype(jnp.bfloat16)


def local(
    queries,
    keys_in,
    values_in,
    ssm_input,
    step_size,
    in_proj_b,
    out_proj_c,
    decay_rate,
    skip_gain,
    doc_lengths,
):
    block_len = ssm_input.shape[0]
    position = lax.axis_index("ctx")
    first = position * block_len
    q_heads, k_heads, v_heads = (
        lax.all_to_all(queries, "head", split_axis=1, concat_axis=0, tiled=True),
        lax.all_to_all(keys_in, "head", split_axis=1, concat_axis=0, tiled=True),
        lax.all_to_all(values_in, "head", split_axis=1, concat_axis=0, tiled=True),
    )
    heads_here = q_heads.shape[1] // ATT_HD
    earlier = []
    for back in (1, 2, 3):
        earlier.append(shifted((k_heads, v_heads), "ctx", back))
    key_rows = jnp.concatenate([earlier[2][0], earlier[1][0], earlier[0][0], k_heads], axis=0)
    val_rows = jnp.concatenate([earlier[2][1], earlier[1][1], earlier[0][1], v_heads], axis=0)
    qpos = first + jnp.arange(block_len)
    kpos = first - 3 * block_len + jnp.arange(4 * block_len)
    qdoc = doc_of(qpos, doc_lengths)
    kdoc = doc_of(kpos, doc_lengths)
    mixed = attend(q_heads, key_rows, val_rows, qpos, kpos, qdoc, kdoc, heads_here)
    attn = lax.all_to_all(mixed, "head", split_axis=0, concat_axis=1, tiled=True)
    state_width = in_proj_b.shape[1] // M_GROUPS
    group_index = lax.axis_index("head") // (lax.axis_size("head") // M_GROUPS)
    b_group = lax.dynamic_slice_in_dim(in_proj_b, group_index * state_width, state_width, 1)
    c_group = lax.dynamic_slice_in_dim(out_proj_c, group_index * state_width, state_width, 1)
    doc_before = doc_of(jnp.reshape(first - 1, (1,)), doc_lengths)[0]
    outs, final, link_all, cumul = ssd_local(
        ssm_input, step_size, b_group, c_group, decay_rate, qdoc, doc_before, SCAN_LEN
    )
    heads_ssm = step_size.shape[1]
    identity = (jnp.ones((heads_ssm,), jnp.float32), jnp.zeros_like(final))
    incoming = entering((link_all, final), "ctx", combine_states, identity)[1]
    carried = (qdoc == doc_before).astype(jnp.float32)
    entry = jnp.exp(cumul) * carried[:, None]
    extra = entry[:, :, None] * jnp.einsum(
        "tn,hnp->thp", c_group.astype(jnp.float32), incoming, precision=lax.Precision.HIGHEST
    )
    width = ssm_input.shape[1] // heads_ssm
    skip = jnp.repeat(skip_gain, width)
    ssm = (
        outs + jnp.reshape(extra, outs.shape) + skip[None, :] * ssm_input.astype(jnp.float32)
    ).astype(jnp.bfloat16)
    return (attn, ssm)


def solution(mesh):
    return jax.shard_map(
        local,
        mesh=mesh,
        in_specs=(
            P(("ctx", "head"), None),
            P(("ctx", "head"), None),
            P(("ctx", "head"), None),
            P("ctx", "head"),
            P("ctx", "head"),
            P("ctx", None),
            P("ctx", None),
            P("head"),
            P("head"),
            P(),
        ),
        out_specs=(P(("ctx", "head"), None), P("ctx", "head")),
        check_vma=False,
    )
```

profile of v0, /device:TPU:111, one launch (start us, length us, event | category | flops | bytes accessed | tf_op | source)
XLA Modules:
  0.0 601.0 jit_solution(11301066665379804941)
XLA Ops:
  21.7 126.7 %while.26 = (s32[]{:T(128)}, f32[28,64,64]{2,1,0:T(8,128)}, f32[2,256,28,64]{1,0,3,2:T(2,128)}, f32[2,256,28]{1,0,2:T(2,128)S(1)}, f32[2,28]{1,0:T(2,128)S(1)}, ...) while((s32[]{:T(128)}, f32[28,64,64]{2,1,0:T(8,128)}, ...), condition=%wide.region_9.10_spmd.clone, body=%wide.region_8.9_spmd.clone.sunk | while | flops 2133470208 | bytes 24811856 | solution.py:85
  21.9 4.0 constant_dynamic-slice_fusion.10
  36.7 8.5 %fusion.108 = f32[1,256,28,64]{1,3,2,0:T(8,128)S(1)} fusion(f32[256,28,64]{0,2,1:T(8,128)S(1)} %bitcast.186, f32[28,256]{1,0:T(8,128)S(1)} %bitcast.209, f32[256,256]{1,0:T(8,128)S(1)} %fusion.106, f32[28,256]{1,0:T(8,128)S(1)} %get-tuple-element.412, pred[256,256]{1,0:T(8,128)(4,1)S(1)} %fusion.107, ...), kind=kOutput, calls=%fused_computation.18.clone.1 | convolution fusion | flops 1419378688 | bytes 5918720 | tf_op jit(solution)/shard_map/while/body/eval_jaxpr/hts,shp->thp/dot_general | solution.py:63
  47.1 37.4 %dynamic_update_slice.6 = f32[2,256,28,64]{1,0,3,2:T(2,128)} dynamic-update-slice(f32[2,256,28,64]{1,0,3,2:T(2,128)} %get-tuple-element.430, f32[1,256,28,64]{1,0,3,2:T(1,128)S(1)} %copy.309, s32[]{:T(128)S(6)} %copy.314, s32[]{:T(128)} %constant.89.clone.1..sunk.1, s32[]{:T(128)} %constant.89.clone.1..sunk.1, s32[]{:T(128)} %constant.89.clone.1..sunk.1) | dynamic-update-slice | bytes 3670020 | tf_op jit(solution)/shard_map/while/body/jit(dynamic_update_index_in_dim)/dynamic_update_slice | solution.py:85
  84.5 4.0 constant_dynamic-slice_fusion.10
  100.5 8.5 %fusion.108 = f32[1,256,28,64]{1,3,2,0:T(8,128)S(1)} fusion(f32[256,28,64]{0,2,1:T(8,128)S(1)} %bitcast.186, f32[28,256]{1,0:T(8,128)S(1)} %bitcast.209, f32[256,256]{1,0:T(8,128)S(1)} %fusion.106, f32[28,256]{1,0:T(8,128)S(1)} %get-tuple-element.412, pred[256,256]{1,0:T(8,128)(4,1)S(1)} %fusion.107, ...), kind=kOutput, calls=%fused_computation.18.clone.1 | convolution fusion | flops 1419378688 | bytes 5918720 | tf_op jit(solution)/shard_map/while/body/eval_jaxpr/hts,shp->thp/dot_general | solution.py:63
  110.9 37.4 %dynamic_update_slice.6 = f32[2,256,28,64]{1,0,3,2:T(2,128)} dynamic-update-slice(f32[2,256,28,64]{1,0,3,2:T(2,128)} %get-tuple-element.430, f32[1,256,28,64]{1,0,3,2:T(1,128)S(1)} %copy.309, s32[]{:T(128)S(6)} %copy.314, s32[]{:T(128)} %constant.89.clone.1..sunk.1, s32[]{:T(128)} %constant.89.clone.1..sunk.1, s32[]{:T(128)} %constant.89.clone.1..sunk.1) | dynamic-update-slice | bytes 3670020 | tf_op jit(solution)/shard_map/while/body/jit(dynamic_update_index_in_dim)/dynamic_update_slice | solution.py:85
  148.5 3.9 copy.230
  152.4 25.8 %all_to_all.70 = bf16[128,4,1792]{0,2,1:T(8,128)(2,1)S(1)} all-to-all(bf16[128,4,1792]{0,2,1:T(8,128)(2,1)} %bitcast.193), channel_id=1, replica_groups=mesh['ctx'=32,'head'=4] {'head'}, dimensions={1} | all-to-all | bytes 3670016 | tf_op jit(solution)/shard_map/all_to_all | solution.py:134
  182.0 3.9 copy.223
  185.8 5.7 all-to-all-start
  194.1 17.5 %all-to-all-done = bf16[128,4,1792]{0,2,1:T(8,128)(2,1)} async-done(((bf16[128,4,1792]{0,2,1:T(8,128)(2,1)}), bf16[128,4,1792]{0,2,1:T(8,128)(2,1)}, u32[]{:S(2)}, u32[]{:S(2)}) %all-to-all-start) | async-done | bytes 1835040 | tf_op jit(solution)/shard_map/all_to_all | solution.py:135
  211.6 3.9 copy.224
  219.4 3.9 copy.236
  223.3 5.6 all-to-all-start.2
  230.6 11.4 %all-to-all-done.2 = bf16[128,4,1792]{0,2,1:T(8,128)(2,1)} async-done(((bf16[128,4,1792]{0,2,1:T(8,128)(2,1)}), bf16[128,4,1792]{0,2,1:T(8,128)(2,1)}, u32[]{:S(2)}, u32[]{:S(2)}) %all-to-all-start.2) | async-done | bytes 1835040 | tf_op jit(solution)/shard_map/all_to_all | solution.py:133
  242.0 9.7 %copy.237 = bf16[4,128,1792]{1,0,2:T(4,128)(2,1)} copy(bf16[4,128,1792]{1,2,0:T(8,128)(2,1)} %bitcast.20) | data formatting | bytes 3670016 | tf_op jit(solution)/shard_map/all_to_all | solution.py:133
  251.7 4.1 reshape.290
  255.8 9.4 %copy.235 = bf16[4,128,1792]{1,0,2:T(4,128)(2,1)} copy(bf16[4,128,1792]{1,2,0:T(8,128)(2,1)S(1)} %bitcast.187) | data formatting | bytes 3670016 | tf_op jit(solution)/shard_map/all_to_all | solution.py:134
  265.2 4.2 concatenate.38
  269.4 9.2 %copy.228 = bf16[4,128,1792]{1,0,2:T(4,128)(2,1)S(1)} copy(bf16[4,128,1792]{1,2,0:T(8,128)(2,1)} %bitcast.9) | data formatting | bytes 3670016 | tf_op jit(solution)/shard_map/all_to_all | solution.py:135
  284.1 35.1 %collective-permute-done.4 = bf16[512,1792]{1,0:T(8,128)(2,1)} collective-permute-done((bf16[512,1792]{1,0:T(8,128)(2,1)}, bf16[512,1792]{1,0:T(8,128)(2,1)}, u32[]{:S(2)}, u32[]{:S(2)}) %collective-permute-start.4) | collective-permute-done | bytes 1835040 | tf_op jit(solution)/shard_map/ppermute | solution.py:14
  323.1 7.3 %collective-permute-done.3 = bf16[512,1792]{1,0:T(8,128)(2,1)} collective-permute-done((bf16[512,1792]{1,0:T(8,128)(2,1)}, bf16[512,1792]{1,0:T(8,128)(2,1)}, u32[]{:S(2)}, u32[]{:S(2)}) %collective-permute-start.3) | collective-permute-done | bytes 1835040 | tf_op jit(solution)/shard_map/ppermute | solution.py:14
  338.1 59.8 %collective-permute-done.1 = bf16[512,1792]{1,0:T(8,128)(2,1)} collective-permute-done((bf16[512,1792]{1,0:T(8,128)(2,1)}, bf16[512,1792]{1,0:T(8,128)(2,1)}, u32[]{:S(2)}, u32[]{:S(2)}) %collective-permute-start.1) | collective-permute-done | bytes 1835040 | tf_op jit(solution)/shard_map/ppermute | solution.py:14
  403.3 3.9 copy.225
  407.2 15.2 %fusion.55 = f32[8,2048,512]{2,1,0:T(8,128)} fusion(bf16[512,8,224]{0,2,1:T(8,128)(2,1)S(1)} %copy-done.3, bf16[512,8,224]{0,2,1:T(8,128)(2,1)} %concatenate.38, bf16[512,8,224]{0,2,1:T(8,128)(2,1)} %bitcast.194, bf16[512,8,224]{0,2,1:T(8,128)(2,1)} %bitcast.195, bf16[512,8,224]{0,2,1:T(8,128)(2,1)} %bitcast.196), kind=kOutput, calls=%fused_computation.72 | convolution fusion | flops 3787456512 | bytes 42729472 | tf_op jit(solution)/shard_map/qhd,khd->hqk/dot_general | solution.py:101
  422.4 30.7 %fusion.76 = (f32[8,512]{1,0:T(8,128)S(1)}, bf16[8,512,2048]{1,2,0:T(8,128)(2,1)}) fusion(f32[8,2048,512]{2,1,0:T(8,128)} %fusion.55, pred[512,2048]{0,1:T(8,128)(4,1)S(1)} %compare_and_fusion), kind=kOutput, calls=%fused_computation.110 | output fusion | flops 67110912 | bytes 51396608 | tf_op jit(solution)/shard_map/sub | solution.py:107
  453.1 10.6 %fusion.65 = bf16[512,8,224]{0,2,1:T(8,128)(2,1)} fusion(bf16[8,512,2048]{1,2,0:T(8,128)(2,1)} %get-tuple-element.296, bf16[512,8,224]{0,2,1:T(8,128)(2,1)S(1)} %copy-done.4, bf16[512,8,224]{0,2,1:T(8,128)(2,1)} %bitcast.205, bf16[512,8,224]{0,2,1:T(8,128)(2,1)} %bitcast.206, bf16[512,8,224]{0,2,1:T(8,128)(2,1)} %bitcast.207, f32[512,8]{0,1:T(8,128)S(1)} %bitcast.223), kind=kOutput, calls=%fused_computation.85 | convolution fusion | flops 3789291520 | bytes 25968640 | tf_op jit(solution)/shard_map/hqk,khd->qhd/dot_general | solution.py:111
  468.4 4.7 all-to-all-start.3
  473.7 4.2 copy.274
  478.9 60.2 %all-gather.1 = f32[32,1,28]{2,1,0:T(1,128)S(1)} all-gather(f32[1,1,28]{2,1,0:T(1,128)S(1)} %bitcast.221), channel_id=1, replica_groups=mesh['ctx'=32,'head'=4] {'ctx'}, dimensions={0}, use_global_device_ids=true | all-gather | bytes 3696 | tf_op jit(solution)/shard_map/all_gather | solution.py:19
  542.1 44.3 %while.25 = (s32[]{:T(128)}, f32[28,64,64]{2,1,0:T(8,128)S(1)}, s32[]{:T(128)}, f32[32,28]{1,0:T(8,128)S(1)}, f32[32,28,64,64]{3,2,1,0:T(8,128)}, /*index=5*/s32[]{:T(128)}, s32[]{:T(128)}, s32[]{:T(128)}) while((s32[]{:T(128)}, f32[28,64,64]{2,1,0:T(8,128)S(1)}, s32[]{:T(128)}, f32[32,28]{1,0:T(8,128)S(1)}, f32[32,28,64,64]{3,2,1,0:T(8,128)}, ...), condition=%wide.region_11.12_spmd, body=%wide.region_10.11_spmd.sunk | while | flops 229381 | bytes 1376727 | solution.py:27
  (192 shorter events, 131.4 us)
Async XLA Ops:
  7.2 534.9 %all-gather.4.cloned.1.call-start = ((), (), s32[]{:S(2)}) async-start(), calls=%async_computation.4 | async-start | bytes 30277632 | tf_op jit(solution)/shard_map/all_gather | solution.py:19
  10.4 4.6 copy-start.7
  15.0 6.5 %copy-start.5 = (bf16[512,64]{1,0:T(8,128)(2,1)}, bf16[512,64]{1,0:T(8,128)(2,1)S(1)}, u32[]{:S(2)}) copy-start(bf16[512,64]{1,0:T(8,128)(2,1)S(1)} %get-tuple-element.297) | copy-start | bytes 196612
  18.0 3.7 copy-start
  180.7 37.4 %collective-permute-start.5 = (bf16[512,1792]{1,0:T(8,128)(2,1)}, bf16[512,1792]{1,0:T(8,128)(2,1)}, u32[]{:S(2)}, u32[]{:S(2)}) collective-permute-start(bf16[512,1792]{1,0:T(8,128)(2,1)} %bitcast.199), channel_id=1, source_target_pairs={{0,4},{4,8},{8,12},{12,16},{16,20},{20,24},{24,28},{28,32},{32,36}... | collective-permute-start | bytes 5505032 | tf_op jit(solution)/shard_map/ppermute | solution.py:14
  185.8 25.8 %all-to-all-start = ((bf16[128,4,1792]{0,2,1:T(8,128)(2,1)}), bf16[128,4,1792]{0,2,1:T(8,128)(2,1)}, u32[]{:S(2)}, u32[]{:S(2)}) async-start(bf16[128,4,1792]{0,2,1:T(8,128)(2,1)} %bitcast.192), calls=%async_computation | async-start | bytes 3670016 | tf_op jit(solution)/shard_map/all_to_all | solution.py:135
  191.5 127.7 %collective-permute-start.4 = (bf16[512,1792]{1,0:T(8,128)(2,1)}, bf16[512,1792]{1,0:T(8,128)(2,1)}, u32[]{:S(2)}, u32[]{:S(2)}) collective-permute-start(bf16[512,1792]{1,0:T(8,128)(2,1)} %bitcast.200), channel_id=1, source_target_pairs={{0,8},{4,12},{8,16},{12,20},{16,24},{20,28},{24,32},{28,36},{32,40... | collective-permute-start | bytes 5505032 | tf_op jit(solution)/shard_map/ppermute | solution.py:14
  192.8 137.6 %collective-permute-start.3 = (bf16[512,1792]{1,0:T(8,128)(2,1)}, bf16[512,1792]{1,0:T(8,128)(2,1)}, u32[]{:S(2)}, u32[]{:S(2)}) collective-permute-start(bf16[512,1792]{1,0:T(8,128)(2,1)} %bitcast.201), channel_id=1, source_target_pairs={{0,12},{4,16},{8,20},{12,24},{16,28},{20,32},{24,36},{28,40},{32,4... | collective-permute-start | bytes 5505032 | tf_op jit(solution)/shard_map/ppermute | solution.py:14
  215.5 118.7 %collective-permute-start.2 = (bf16[512,1792]{1,0:T(8,128)(2,1)}, bf16[512,1792]{1,0:T(8,128)(2,1)}, u32[]{:S(2)}, u32[]{:S(2)}) collective-permute-start(bf16[512,1792]{1,0:T(8,128)(2,1)} %bitcast.202), channel_id=1, source_target_pairs={{0,4},{4,8},{8,12},{12,16},{16,20},{20,24},{24,28},{28,32},{32,36}... | collective-permute-start | bytes 5505032 | tf_op jit(solution)/shard_map/ppermute | solution.py:14
  216.8 181.1 %collective-permute-start.1 = (bf16[512,1792]{1,0:T(8,128)(2,1)}, bf16[512,1792]{1,0:T(8,128)(2,1)}, u32[]{:S(2)}, u32[]{:S(2)}) collective-permute-start(bf16[512,1792]{1,0:T(8,128)(2,1)} %bitcast.203), channel_id=1, source_target_pairs={{0,8},{4,12},{8,16},{12,20},{16,24},{20,28},{24,32},{28,36},{32,40... | collective-permute-start | bytes 5505032 | tf_op jit(solution)/shard_map/ppermute | solution.py:14
  218.1 185.2 %collective-permute-start = (bf16[512,1792]{1,0:T(8,128)(2,1)}, bf16[512,1792]{1,0:T(8,128)(2,1)}, u32[]{:S(2)}, u32[]{:S(2)}) collective-permute-start(bf16[512,1792]{1,0:T(8,128)(2,1)} %bitcast.204), channel_id=1, source_target_pairs={{0,12},{4,16},{8,20},{12,24},{16,28},{20,32},{24,36},{28,40},{32,4... | collective-permute-start | bytes 5505032 | tf_op jit(solution)/shard_map/ppermute | solution.py:14
  223.3 18.7 %all-to-all-start.2 = ((bf16[128,4,1792]{0,2,1:T(8,128)(2,1)}), bf16[128,4,1792]{0,2,1:T(8,128)(2,1)}, u32[]{:S(2)}, u32[]{:S(2)}) async-start(bf16[128,4,1792]{0,2,1:T(8,128)(2,1)} %bitcast.191), calls=%async_computation.2 | async-start | bytes 3670016 | tf_op jit(solution)/shard_map/all_to_all | solution.py:133
  338.1 69.1 %copy-start.3 = (bf16[512,8,224]{0,2,1:T(8,128)(2,1)S(1)}, bf16[512,8,224]{0,2,1:T(8,128)(2,1)}, u32[]{:S(2)}) copy-start(bf16[512,8,224]{0,2,1:T(8,128)(2,1)} %reshape.290) | copy-start | bytes 5505028
  422.4 30.7 %copy-start.4 = (bf16[512,8,224]{0,2,1:T(8,128)(2,1)S(1)}, bf16[512,8,224]{0,2,1:T(8,128)(2,1)}, u32[]{:S(2)}) copy-start(bf16[512,8,224]{0,2,1:T(8,128)(2,1)} %concatenate.33) | copy-start | bytes 5505028
  468.4 70.8 %all-to-all-start.3 = ((bf16[4,128,1792]{1,2,0:T(8,128)(2,1)}), bf16[4,128,1792]{1,2,0:T(8,128)(2,1)S(1)}, u32[]{:S(2)}, u32[]{:S(2)}) async-start(bf16[4,128,1792]{1,2,0:T(8,128)(2,1)} %copy.239), calls=%async_computation.3 | async-start | bytes 3670016 | tf_op jit(solution)/shard_map/all_to_all | solution.py:148
  473.7 4.9 copy-start.9
  473.7 5.1 copy-start.8
  542.1 44.6 %copy-start.6 = (bf16[512,64]{1,0:T(8,128)(2,1)S(1)}, bf16[512,64]{1,0:T(8,128)(2,1)}, u32[]{:S(2)}) copy-start(bf16[512,64]{1,0:T(8,128)(2,1)} %copy-done.5) | copy-start | bytes 196612
  588.4 1.5 copy-start.1
  588.4 2.6 copy-start.2
Sparse Core Ops, SparseCore 0:
  148.6 157.5 all-gather.3
where the time goes:
time: 612 us; the launch traced here: 601 us
  local copies, waits for them, and re-layouts  199 us (33%)
  waiting for transfers between devices  133 us (22%)
  blocking collectives  86 us (14%)
  other arithmetic  85 us (14%)
  matrix products  54.7 us (9%)
  starting transfers between devices  23.7 us (4%)
  between operations  15.9 us (3%)
    ppermute x6, waiting for transfers between devices, shifted(): return lax.ppermute(block, axis, route)  104 us
    dynamic_update_slice x4, local copies, waits for them, and re-layouts, ssd_local(): final, outs = lax.scan(advance, start, pieces)  78.5 us
    all_gather x1, blocking collectives, entering(): gathered = jax.tree.map(lambda a: lax.all_gather(a, axis), part)  60.2 us
    add x31, other arithmetic, combine_states(): later[0][:, None, None] * earlier[1] + later[1]  42.9 us
    sub x1, other arithmetic, attend(): weights = jnp.where(kept[None], jnp.exp(scores - top), 0.0)  30.7 us
    unnamed x33, local copies, waits for them, and re-layouts  27.3 us
    all_to_all x1, blocking collectives, local(): lax.all_to_all(keys_in, 'head', split_axis=1, concat_axis=0, tiled=True)  25.8 us
    ppermute x6, local copies, waits for them, and re-layouts, shifted(): return lax.ppermute(block, axis, route)  23 us
  transfers between devices with their start and end apart: 10, of which 6 were waited for; matrix products, arithmetic and copies ran while one was open for 25% of the time, Pallas kernels for 0%

commit v1 on v0

v1 whole, which is shorter than its diff:
```python
import functools

import jax
import jax.numpy as jnp
from jax import lax
from jax.experimental import pallas as pl
from jax.experimental.pallas import tpu as pltpu
from jax.sharding import Mesh
from jax.sharding import PartitionSpec as P

ATT_HD = 224
M_HD = 64
M_GROUPS = 2
MOST_DOC = 1536
BLOCK = 128
TILE = 256
PLANE = ("x", "c", "y")
CTX = ("z", "x", "c")

F32 = jnp.float32
BF16 = jnp.bfloat16


def compiler_params(mib=48):
    return pltpu.CompilerParams(vmem_limit_bytes=mib * 1024 * 1024)


def split2(value):
    high = value.astype(BF16)
    return high, (value - high.astype(F32)).astype(BF16)


def split3(value):
    high, rest = value.astype(BF16), None
    rest = value - high.astype(F32)
    middle = rest.astype(BF16)
    return high, middle, (rest - middle.astype(F32)).astype(BF16)


def dot(a, b):
    return jnp.dot(a, b, preferred_element_type=F32)


def turn_kernel(count, parts, *refs):
    sources, out, held, turned = refs[:count], refs[count], refs[count + 1 : 2 * count + 1], refs[2 * count + 1]
    in_sems, out_sems = refs[2 * count + 2 :]
    step = turned.shape[0] // parts
    width = step * ATT_HD

    def arriving(i, part):
        columns = pl.ds(part * width, width)
        return pltpu.make_async_copy(sources[i].at[:, columns], held[i].at[:, columns], in_sems.at[i, part])

    def leaving(part):
        rows = pl.ds(part * step, step)
        return pltpu.make_async_copy(turned.at[rows], out.at[rows], out_sems.at[part])

    for part in range(parts):
        for i in range(count):
            arriving(i, part).start()
    for part in range(parts):
        for i in range(count):
            arriving(i, part).wait()
            block = held[i][:, part * width : (part + 1) * width].T
            turned[part * step : (part + 1) * step, i * ATT_HD : (i + 1) * ATT_HD, :] = jnp.reshape(
                block, (step, ATT_HD, BLOCK)
            )
        leaving(part).start()
    for part in range(parts):
        leaving(part).wait()


def turn(arrays, mib):
    count, parts = len(arrays), 4
    width = arrays[0].shape[1]
    heads = width // ATT_HD
    return pl.pallas_call(
        functools.partial(turn_kernel, count, parts),
        in_specs=[pl.BlockSpec(memory_space=pl.ANY)] * count,
        out_specs=pl.BlockSpec(memory_space=pl.ANY),
        out_shape=jax.ShapeDtypeStruct((heads, count * ATT_HD, BLOCK), BF16),
        scratch_shapes=[pltpu.VMEM((BLOCK, width), BF16)] * count
        + [
            pltpu.VMEM((heads, count * ATT_HD, BLOCK), BF16),
            pltpu.SemaphoreType.DMA((count, parts)),
            pltpu.SemaphoreType.DMA((parts,)),
        ],
        compiler_params=compiler_params(mib),
        cost_estimate=pl.CostEstimate(flops=0, bytes_accessed=4 * BLOCK * width * count, transcendentals=0),
    )(*arrays)


def turn_back_kernel(a_ref, out_ref):
    heads = a_ref.shape[0]
    out_ref[...] = jnp.reshape(a_ref[...], (heads * ATT_HD, BLOCK)).T


def turn_back(blocks):
    heads = blocks.shape[0]
    step = 16
    return pl.pallas_call(
        turn_back_kernel,
        grid=(heads // step,),
        in_specs=[pl.BlockSpec((step, ATT_HD, BLOCK), lambda i: (i, 0, 0))],
        out_specs=pl.BlockSpec((BLOCK, step * ATT_HD), lambda i: (0, i)),
        out_shape=jax.ShapeDtypeStruct((BLOCK, heads * ATT_HD), BF16),
        compiler_params=compiler_params(),
        cost_estimate=pl.CostEstimate(flops=0, bytes_accessed=4 * BLOCK * heads * ATT_HD, transcendentals=0),
    )(blocks)


def key_rows_kernel(k_ref, out_ref):
    for i in range(k_ref.shape[0]):
        out_ref[i * BLOCK : (i + 1) * BLOCK, :] = k_ref[i].T


def key_rows(kv_blocks):
    count = kv_blocks.shape[0]
    step = 4
    return pl.pallas_call(
        key_rows_kernel,
        grid=(count // step,),
        in_specs=[pl.BlockSpec((step, ATT_HD, BLOCK), lambda i: (i, 0, 0))],
        out_specs=pl.BlockSpec((step * BLOCK, ATT_HD), lambda i: (i, 0)),
        out_shape=jax.ShapeDtypeStruct((count * BLOCK, ATT_HD), BF16),
        compiler_params=compiler_params(16),
        cost_estimate=pl.CostEstimate(flops=0, bytes_accessed=4 * count * BLOCK * ATT_HD, transcendentals=0),
    )(kv_blocks)


def attend_kernel(
    most, reach_ref, starts_ref, q_ref, own_k, own_v, halo_k, halo_v, o_ref,
    k_rows, v_cols, q_own, o_own, halo_sems, sems, out_sems,
):
    halo = halo_v.shape[0]
    own = q_ref.shape[0]
    per = TILE // BLOCK
    pairs = own // per // 2
    span = 2 * per

    def arriving(p):
        blocks = pl.ds(span * p, span)
        tokens = span * BLOCK
        return (
            pltpu.make_async_copy(
                own_k.at[pl.ds(pl.multiple_of(p * tokens, tokens), tokens)],
                k_rows.at[pl.ds(pl.multiple_of(halo * BLOCK + p * tokens, tokens), tokens)],
                sems.at[0, p],
            ),
            pltpu.make_async_copy(own_v.at[blocks], v_cols.at[pl.ds(halo + span * p, span)], sems.at[1, p]),
            pltpu.make_async_copy(q_ref.at[blocks], q_own.at[blocks], sems.at[2, p]),
        )

    halo_copies = (
        pltpu.make_async_copy(halo_k, k_rows.at[pl.ds(0, halo * BLOCK)], halo_sems.at[0]),
        pltpu.make_async_copy(halo_v, v_cols.at[pl.ds(0, halo)], halo_sems.at[1]),
    )
    for copy in halo_copies:
        copy.start()

    def begin(p, _):
        for copy in arriving(p):
            copy.start()
        return 0

    lax.fori_loop(0, pairs, begin, 0)
    for copy in halo_copies:
        copy.wait()
    factor = 1.4426950408889634 / ATT_HD**0.5
    down = lax.broadcasted_iota(jnp.int32, (TILE, TILE), 0)
    causal = down <= lax.broadcasted_iota(jnp.int32, (TILE, TILE), 1)

    def out_copy(p):
        blocks = pl.ds(2 * per * p, 2 * per)
        return pltpu.make_async_copy(o_own.at[blocks], o_ref.at[blocks], out_sems.at[p])

    def pair(p, _):
        reach = reach_ref[p]
        for copy in arriving(p):
            copy.wait()

        def attend_over(reach):
            first = 2 * p + halo // per + 1 - reach
            rows = pl.multiple_of(first * TILE, TILE)
            for half in range(2):
                j = 2 * p + half
                count = reach + half
                q_t = jnp.concatenate([q_own[per * j + i] for i in range(per)], axis=1)
                start = starts_ref[j]
                scores = []
                for i in range(count):
                    s = dot(k_rows[pl.ds(rows + i * TILE, TILE), :], q_t)
                    kept = down >= start - (j - count + 1 + i) * TILE
                    if i == count - 1:
                        kept = jnp.logical_and(kept, causal)
                    scores.append(jnp.where(kept, s, -1e30))
                top = scores[0]
                for s in scores[1:]:
                    top = jnp.maximum(top, s)
                top = jnp.max(top, axis=0, keepdims=True)
                total = jnp.zeros((TILE, TILE), F32)
                mixed = jnp.zeros((ATT_HD, TILE), F32)
                for i in range(count):
                    weights = jnp.exp2((scores[i] - top) * factor)
                    total = total + weights
                    v_t = jnp.concatenate([v_cols[first * per + i * per + b] for b in range(per)], axis=1)
                    mixed = mixed + dot(v_t, weights.astype(BF16))
                total = jnp.sum(total, axis=0, keepdims=True)
                out = (mixed * (1.0 / total)).astype(BF16)
                for b in range(per):
                    o_own[per * j + b] = out[:, b * BLOCK : (b + 1) * BLOCK]

        for count in range(1, most + 1):
            pl.when(reach == count)(functools.partial(attend_over, count))
        out_copy(p).start()
        return 0

    lax.fori_loop(0, pairs, pair, 0)

    def finish(p, _):
        out_copy(p).wait()
        return 0

    lax.fori_loop(0, pairs, finish, 0)


def attend(q_blocks, own_rows, own_v, halo_rows, halo_v, starts):
    own = own_v.shape[0]
    halo = halo_v.shape[0]
    per = TILE // BLOCK
    tiles = own // per
    most = halo // per + 1
    by_tile = jnp.reshape(starts, (tiles, 1, TILE))
    reach = jnp.arange(0, tiles, 2, dtype=jnp.int32) - by_tile[::2, 0, 0] // TILE + 1
    vmem = pl.BlockSpec(memory_space=pltpu.VMEM)
    anywhere = pl.BlockSpec(memory_space=pl.ANY)
    return pl.pallas_call(
        functools.partial(attend_kernel, most),
        in_specs=[pl.BlockSpec(memory_space=pltpu.SMEM), vmem] + [anywhere] * 5,
        out_specs=anywhere,
        out_shape=jax.ShapeDtypeStruct((own, ATT_HD, BLOCK), BF16),
        scratch_shapes=[
            pltpu.VMEM(((own + halo) * BLOCK, ATT_HD), BF16),
            pltpu.VMEM((own + halo, ATT_HD, BLOCK), BF16),
            pltpu.VMEM((own, ATT_HD, BLOCK), BF16),
            pltpu.VMEM((own, ATT_HD, BLOCK), BF16),
            pltpu.SemaphoreType.DMA((2,)),
            pltpu.SemaphoreType.DMA((3, tiles // 2)),
            pltpu.SemaphoreType.DMA((tiles // 2,)),
        ],
        compiler_params=compiler_params(60),
        cost_estimate=pl.CostEstimate(flops=4_000_000_000, bytes_accessed=8_000_000, transcendentals=4_000_000),
    )(reach, by_tile, q_blocks, own_rows, own_v, halo_rows, halo_v)


def cumulative(rate_ref, step_ref):
    length = step_ref.shape[0]
    decay = -rate_ref[...] * step_ref[...]
    order = lax.broadcasted_iota(jnp.int32, (length, length), 0)
    lower = (lax.broadcasted_iota(jnp.int32, (length, length), 1) <= order).astype(F32).astype(BF16)
    a, b, c = split3(decay)
    return dot(lower, a) + dot(lower, b) + dot(lower, c)


def spread(value, wide_ref):
    return dot(jnp.concatenate(split3(value), axis=1), wide_ref[...])


def state_kernel(first_ref, start_ref, x_ref, step_ref, b_ref, rate_ref, wide_ref, out_ref, weight, passed):
    length = x_ref.shape[0]
    cumul = None

    @pl.when(pl.program_id(0) == 0)
    def _():
        cumul = cumulative(rate_ref, step_ref)
        last = cumul[length - 1 :, :]
        weight[...] = jnp.exp(last - cumul) * step_ref[...]
        linked = jnp.where(start_ref[length - 1 :, :] < first_ref[0], 1.0, 0.0)
        passed[...] = jnp.broadcast_to(jnp.exp(last) * linked, passed.shape)

    last_start = start_ref[length - 1 :, :]
    at = first_ref[0] + lax.broadcasted_iota(jnp.int32, (length, 1), 0)
    same = at >= last_start
    b_same = jnp.where(same, b_ref[...].astype(F32), 0.0).astype(BF16)
    update = spread(weight[...], wide_ref) * x_ref[...].astype(F32)
    high, low = split2(update)
    over = (((0,), (0,)), ((), ()))
    fresh = lax.dot_general(b_same, high, over, preferred_element_type=F32) + lax.dot_general(
        b_same, low, over, preferred_element_type=F32
    )
    states = fresh.shape[0]
    out_ref[:states, :] = fresh
    out_ref[states:, :] = spread(passed[...], wide_ref)


def scan_kernel(
    first_ref, start_ref, x_ref, step_ref, b_ref, c_ref, rate_ref, wide_ref, skip_ref,
    near_ref, far_ref, out_ref, weight, growth, g_high, g_low, c_open,
):
    length = x_ref.shape[0]
    states = b_ref.shape[1]

    @pl.when(pl.program_id(0) == 0)
    def _():
        cumul = cumulative(rate_ref, step_ref)
        growth[...] = jnp.exp(cumul)
        weight[...] = jnp.exp(-cumul) * step_ref[...]
        gram = lax.dot_general(c_ref[...], b_ref[...], (((1,), (1,)), ((), ())), preferred_element_type=F32)
        at = lax.broadcasted_iota(jnp.int32, (length, length), 1)
        kept = jnp.logical_and(
            at <= lax.broadcasted_iota(jnp.int32, (length, length), 0), at + first_ref[0] >= start_ref[...]
        )
        high, low = split2(jnp.where(kept, gram, 0.0))
        g_high[...] = high
        g_low[...] = low
        c_open[...] = jnp.where(start_ref[...] < first_ref[0], c_ref[...].astype(F32), 0.0).astype(BF16)

    x = x_ref[...].astype(F32)
    high, low = split2(spread(weight[...], wide_ref) * x)
    entering = near_ref[:states, :] + near_ref[states : states + 1, :] * far_ref[...]
    e_high, e_low = split2(entering)
    c = c_open[...]
    inner = dot(g_high[...], high) + dot(g_high[...], low) + dot(g_low[...], high) + dot(c, e_high) + dot(c, e_low)
    out_ref[...] = (spread(growth[...], wide_ref) * inner + skip_ref[...] * x).astype(BF16)


def whole(shape):
    return pl.BlockSpec(shape, lambda i: (0,) * len(shape))


def scan_parts(x, step, b_group, c_group, rate, skip, start, first):
    length, width = x.shape
    heads = step.shape[1]
    states = b_group.shape[1]
    chunk = 256
    wide = jnp.repeat(jnp.eye(heads, dtype=BF16), width // heads, axis=1)
    wide = jnp.concatenate([wide] * 3, axis=0)
    rate = rate[None, :]
    start = start[:, None]
    first = jnp.reshape(first, (1,)).astype(jnp.int32)
    smem = pl.BlockSpec(memory_space=pltpu.SMEM)
    columns = lambda rows: pl.BlockSpec((rows, chunk), lambda i: (0, i))
    extra = 8
    state = pl.pallas_call(
        state_kernel,
        grid=(width // chunk,),
        in_specs=[
            smem, whole((length, 1)), columns(length), whole((length, heads)), whole((length, states)),
            whole((1, heads)), columns(3 * heads),
        ],
        out_specs=columns(states + extra),
        out_shape=jax.ShapeDtypeStruct((states + extra, width), F32),
        scratch_shapes=[pltpu.VMEM((length, heads), F32), pltpu.VMEM((extra, heads), F32)],
        compiler_params=compiler_params(16),
        cost_estimate=pl.CostEstimate(flops=2_000_000_000, bytes_accessed=3_000_000, transcendentals=20_000),
    )(first, start, x, step, b_group, rate, wide)

    def finish(near, far):
        return pl.pallas_call(
            scan_kernel,
            grid=(width // chunk,),
            in_specs=[
                smem, whole((length, 1)), columns(length), whole((length, heads)), whole((length, states)),
                whole((length, states)), whole((1, heads)), columns(3 * heads), columns(1),
                columns(states + extra), columns(states),
            ],
            out_specs=columns(length),
            out_shape=jax.ShapeDtypeStruct((length, width), BF16),
            scratch_shapes=[
                pltpu.VMEM((length, heads), F32),
                pltpu.VMEM((length, heads), F32),
                pltpu.VMEM((length, length), BF16),
                pltpu.VMEM((length, length), BF16),
                pltpu.VMEM((length, states), BF16),
            ],
            compiler_params=compiler_params(16),
            cost_estimate=pl.CostEstimate(flops=5_000_000_000, bytes_accessed=6_000_000, transcendentals=40_000),
        )(first, start, x, step, b_group, c_group, rate, wide, jnp.repeat(skip, width // heads)[None, :], near, far)

    return state, finish


def doc_start(positions, doc_lengths):
    begins = jnp.cumsum(doc_lengths) - doc_lengths
    return jnp.max(jnp.where(begins[None, :] <= positions[:, None], begins[None, :], 0), axis=1).astype(jnp.int32)


def exchange(blocks):
    return lax.all_to_all(blocks, PLANE, split_axis=0, concat_axis=0, tiled=True)


def local(
    queries, keys_in, values_in, ssm_input, step_size, in_proj_b, out_proj_c, decay_rate, skip_gain, doc_lengths
):
    together = lax.optimization_barrier
    block_len = ssm_input.shape[0]
    ctx = lax.axis_index(CTX)
    devices = lax.axis_size(CTX)
    planes = lax.axis_size("z")
    plane_tokens = lax.axis_size(PLANE) * BLOCK
    plane_first = lax.axis_index("z") * plane_tokens
    halo_blocks = MOST_DOC // BLOCK
    to_next = [(i, i + 1) for i in range(planes - 1)]
    k = exchange(turn([keys_in], 60))

    first = ctx * block_len
    start = doc_start(first + jnp.arange(block_len), doc_lengths)
    width = in_proj_b.shape[1] // M_GROUPS
    group = lax.axis_index("y") // (lax.axis_size("y") // M_GROUPS)
    b_group = lax.dynamic_slice_in_dim(in_proj_b, group * width, width, 1)
    c_group = lax.dynamic_slice_in_dim(out_proj_c, group * width, width, 1)
    state, finish = scan_parts(ssm_input, step_size, b_group, c_group, decay_rate, skip_gain, start, first)
    starts = doc_start(plane_first + jnp.arange(plane_tokens), doc_lengths) - plane_first
    v_blocks, state, starts = together((turn([values_in], 16), state, starts))

    v = exchange(v_blocks)
    near = lax.ppermute(state, CTX, [(i, i + 1) for i in range(devices - 1)])
    two = state[:width] + state[width : width + 1] * near[:width]
    halo_k = lax.ppermute(k[-halo_blocks:], "z", to_next)
    own_rows = key_rows(k)
    halo_rows = key_rows(halo_k)
    q_blocks, own_rows, halo_rows = together((turn([queries], 16), own_rows, halo_rows))

    q = exchange(q_blocks)
    halo_v = lax.ppermute(v[-halo_blocks:], "z", to_next)
    q, halo_v, two = together((q, halo_v, two))

    far = lax.ppermute(two, CTX, [(i, i + 2) for i in range(devices - 2)])
    o_blocks, far = together((attend(q, own_rows, v, halo_rows, halo_v, starts), far))

    return turn_back(exchange(o_blocks)), finish(near, far)


def solution(mesh):
    ctx, head = mesh.devices.shape
    inner = Mesh(mesh.devices.reshape(4, ctx // 8, 2, head), ("z", "x", "c", "y"))
    everywhere = P(("z", "x", "c", "y"), None)
    return jax.shard_map(
        local,
        mesh=inner,
        in_specs=(
            everywhere, everywhere, everywhere,
            P(CTX, "y"), P(CTX, "y"), P(CTX, None), P(CTX, None), P("y"), P("y"), P(),
        ),
        out_specs=(everywhere, P(CTX, "y")),
        check_vma=False,
    )
```

time: 612 us -> 157 us (0.26)
  the two profiles are of different devices: /device:TPU:111 before, /device:TPU:64 now
where the time goes in v1:
time: 157 us
  waiting for transfers between devices  61 us (39%)
  Pallas kernels  40.8 us (26%)
  starting transfers between devices  36.8 us (23%)
  local copies, waits for them, and re-layouts  15.3 us (10%)
  other arithmetic  1.98 us (1%)
    all_to_all x4, waiting for transfers between devices, exchange(): lax.all_to_all(blocks, PLANE, split_axis=0, concat_axis=0, tiled=True)  30.5 us
    all_to_all x4, starting transfers between devices, exchange(): lax.all_to_all(blocks, PLANE, split_axis=0, concat_axis=0, tiled=True)  25.6 us
    ppermute x1, waiting for transfers between devices, local(): near = lax.ppermute(state, CTX, [(i, i + 1) for i in range(devices - 1)])  21.9 us
    pallas_call x1, Pallas kernels, attend(): pl.pallas_call(functools.partial(attend_kernel, most), in_specs=[pl.Block...  15.4 us
    unnamed x45, local copies, waits for them, and re-layouts  12.1 us
    pallas_call x1, Pallas kernels, finish(): pl.pallas_call(scan_kernel, grid=(width // chunk,), in_specs=[smem, whole...  9.88 us
    ppermute x1, waiting for transfers between devices, local(): halo_k = lax.ppermute(k[-halo_blocks:], 'z', to_next)  8.66 us
    pallas_call x3, Pallas kernels, turn(): pl.pallas_call(functools.partial(turn_kernel, count, parts), in_specs=[pl...  6.64 us
  transfers between devices with their start and end apart: 8, of which 5 were waited for; matrix products, arithmetic and copies ran while one was open for 3% of the time, Pallas kernels for 23%

profile of v1, /device:TPU:64, one launch (start us, length us, event | category | flops | bytes accessed | tf_op | source)
XLA Modules:
  0.0 157.0 jit_solution(15527791897622544968)
XLA Ops:
  0.6 2.6 %shard_map.116 = bf16[32,224,128]{2,1,0:T(8,128)(2,1)} custom-call(bf16[128,7168]{1,0:T(8,128)(2,1)} %refs_0_.5), custom_call_target="tpu_custom_call" | custom-call | bytes 3670016 | tf_op jit(solution)/shard_map/pallas_call | solution.py:77
  3.2 7.3 %all-to-all-start = ((bf16[32,224,128]{2,1,0:T(8,128)(2,1)}), bf16[32,224,128]{2,1,0:T(8,128)(2,1)S(1)}, u32[]{:S(2)}, u32[]{:S(2)}) async-start(bf16[32,224,128]{2,1,0:T(8,128)(2,1)} %shard_map.116), calls=%async_computation | async-start | bytes 3670016 | tf_op jit(solution)/shard_map/all_to_all | solution.py:389
  10.6 1.5 copy-done.4
  12.1 2.0 %shard_map.113 = bf16[32,224,128]{2,1,0:T(8,128)(2,1)S(1)} custom-call(bf16[128,7168]{1,0:T(8,128)(2,1)S(1)} %copy-done.4), custom_call_target="tpu_custom_call" | custom-call | bytes 3670016 | tf_op jit(solution)/shard_map/pallas_call | solution.py:77
  14.1 1.2 copy-done.1
  15.8 0.9 copy.21.start_ref
  17.7 0.9 copy-done.9
  18.7 1.5 copy-done.11
  20.2 4.7 %shard_map.114 = f32[72,1792]{1,0:T(8,128)S(1)} custom-call(s32[1]{0:T(128)} %bitcast.first_ref, s32[512,1]{1,0:T(8,128)S(1)} %copy-done.9, bf16[512,1792]{1,0:T(8,128)(2,1)S(1)} %copy-done.11, f32[512,28]{1,0:T(8,128)S(1)} %copy.22.step_ref, bf16[512,64]{1,0:T(8,128)(2,1)S(1)} %constant_dynamic-slice_fusion.1.b_ref, f32[1,28]{1,0:T(1,128)S(1)} %bitcast.5, ...), custom_call_target="tpu_custom_call" | custom-call | flops 2000000000 | bytes 3000000 | tf_op jit(solution)/shard_map/pallas_call | solution.py:344
  24.9 11.3 %all-to-all-done.k_ref = bf16[32,224,128]{2,1,0:T(8,128)(2,1)S(1)} async-done(((bf16[32,224,128]{2,1,0:T(8,128)(2,1)}), bf16[32,224,128]{2,1,0:T(8,128)(2,1)S(1)}, u32[]{:S(2)}, u32[]{:S(2)}) %all-to-all-start) | async-done | bytes 1835040 | tf_op jit(solution)/shard_map/all_to_all | solution.py:389
  36.2 4.7 %all-to-all-start.2 = ((bf16[32,224,128]{2,1,0:T(8,128)(2,1)}), bf16[32,224,128]{2,1,0:T(8,128)(2,1)}, u32[]{:S(2)}, u32[]{:S(2)}) async-start(bf16[32,224,128]{2,1,0:T(8,128)(2,1)} %copy-done.1), calls=%async_computation.2 | async-start | bytes 3670016 | tf_op jit(solution)/shard_map/all_to_all | solution.py:389
  41.0 3.5 %collective-permute-start = (bf16[12,224,128]{2,1,0:T(8,128)(2,1)S(1)}, bf16[12,224,128]{2,1,0:T(8,128)(2,1)S(1)}, u32[]{:S(2)}, u32[]{:S(2)}) collective-permute-start(bf16[12,224,128]{2,1,0:T(8,128)(2,1)S(1)} %slice.24), channel_id=1, source_target_pairs={{0,32},{32,64},{64,96},{1,33},{33,65},{65,97},{2,34},{34,66},{66,9... | collective-permute-start | bytes 2064392 | tf_op jit(solution)/shard_map/ppermute | solution.py:419
  44.6 1.5 copy-done.5
  46.0 2.0 %shard_map.115 = bf16[32,224,128]{2,1,0:T(8,128)(2,1)S(1)} custom-call(bf16[128,7168]{1,0:T(8,128)(2,1)S(1)} %copy-done.5), custom_call_target="tpu_custom_call" | custom-call | bytes 3670016 | tf_op jit(solution)/shard_map/pallas_call | solution.py:77
  48.1 1.2 copy-done.2
  49.3 1.0 shard_map.117.own_k
  50.4 1.3 copy-done.3
  51.7 8.7 %collective-permute-done.k_ref = bf16[12,224,128]{2,1,0:T(8,128)(2,1)S(1)} collective-permute-done((bf16[12,224,128]{2,1,0:T(8,128)(2,1)S(1)}, bf16[12,224,128]{2,1,0:T(8,128)(2,1)S(1)}, u32[]{:S(2)}, u32[]{:S(2)}) %collective-permute-start) | collective-permute-done | bytes 688160 | tf_op jit(solution)/shard_map/ppermute | solution.py:419
  60.8 5.8 %all-to-all-done.2.own_v = bf16[32,224,128]{2,1,0:T(8,128)(2,1)} async-done(((bf16[32,224,128]{2,1,0:T(8,128)(2,1)}), bf16[32,224,128]{2,1,0:T(8,128)(2,1)}, u32[]{:S(2)}, u32[]{:S(2)}) %all-to-all-start.2) | async-done | bytes 1835040 | tf_op jit(solution)/shard_map/all_to_all | solution.py:389
  66.5 4.7 %all-to-all-start.1 = ((bf16[32,224,128]{2,1,0:T(8,128)(2,1)}), bf16[32,224,128]{2,1,0:T(8,128)(2,1)}, u32[]{:S(2)}, u32[]{:S(2)}) async-start(bf16[32,224,128]{2,1,0:T(8,128)(2,1)} %copy-done.2), calls=%async_computation.1 | async-start | bytes 3670016 | tf_op jit(solution)/shard_map/all_to_all | solution.py:389
  71.3 2.0 %collective-permute-start.2 = (f32[72,1792]{1,0:T(8,128)S(1)}, f32[72,1792]{1,0:T(8,128)S(1)}, u32[]{:S(2)}, u32[]{:S(2)}) collective-permute-start(f32[72,1792]{1,0:T(8,128)S(1)} %shard_map.114), channel_id=1, source_target_pairs={{0,4},{4,8},{8,12},{12,16},{16,20},{20,24},{24,28},{28,32},{32,36}... | collective-permute-start | bytes 1548296 | tf_op jit(solution)/shard_map/ppermute | solution.py:417
  73.3 1.1 slice.25
  74.4 3.5 %collective-permute-start.1 = (bf16[12,224,128]{2,1,0:T(8,128)(2,1)S(1)}, bf16[12,224,128]{2,1,0:T(8,128)(2,1)S(1)}, u32[]{:S(2)}, u32[]{:S(2)}) collective-permute-start(bf16[12,224,128]{2,1,0:T(8,128)(2,1)S(1)} %slice.25), channel_id=1, source_target_pairs={{0,32},{32,64},{64,96},{1,33},{33,65},{65,97},{2,34},{34,66},{66,9... | collective-permute-start | bytes 2064392 | tf_op jit(solution)/shard_map/ppermute | solution.py:425
  78.3 21.9 %collective-permute-done.2.near_ref = f32[72,1792]{1,0:T(8,128)S(1)} collective-permute-done((f32[72,1792]{1,0:T(8,128)S(1)}, f32[72,1792]{1,0:T(8,128)S(1)}, u32[]{:S(2)}, u32[]{:S(2)}) %collective-permute-start.2) | collective-permute-done | bytes 516128 | tf_op jit(solution)/shard_map/ppermute | solution.py:417
  101.0 2.1 %collective-permute-start.3 = (f32[64,1792]{1,0:T(8,128)}, f32[64,1792]{1,0:T(8,128)S(1)}, u32[]{:S(2)}, u32[]{:S(2)}) collective-permute-start(f32[64,1792]{1,0:T(8,128)} %fusion), channel_id=1, source_target_pairs={{0,8},{4,12},{8,16},{12,20},{16,24},{20,28},{24,32},{28,36},{32,40... | collective-permute-start | bytes 1376264 | tf_op jit(solution)/shard_map/ppermute | solution.py:428
  103.6 15.4 %shard_map.119 = bf16[32,224,128]{2,1,0:T(8,128)(2,1)} custom-call(s32[8]{0:T(128)} %subtract_add_fusion.reach_ref, s32[16,1,256]{2,1,0:T(1,128)} %bitcast.8, bf16[32,224,128]{2,1,0:T(8,128)(2,1)} %all-to-all-done.1.q_ref, bf16[4096,224]{1,0:T(8,128)(2,1)} %copy-done.3, bf16[32,224,128]{2,1,0:T(8,128)(2,1)} %all-to-all-done.2.own_v, ...), custom_call_target="tpu_custom_call" | custom-call | flops 4000000000 | bytes 8000000 | tf_op jit(solution)/shard_map/pallas_call | solution.py:237
  119.9 8.8 %all-to-all-start.3 = ((bf16[32,224,128]{2,1,0:T(8,128)(2,1)}), bf16[32,224,128]{2,1,0:T(8,128)(2,1)}, u32[]{:S(2)}, u32[]{:S(2)}) async-start(bf16[32,224,128]{2,1,0:T(8,128)(2,1)} %shard_map.119), calls=%async_computation.3 | async-start | bytes 3670016 | tf_op jit(solution)/shard_map/all_to_all | solution.py:389
  129.0 0.9 copy-done.10
  130.0 1.0 copy-done.14
  131.0 9.9 %shard_map.121 = bf16[512,1792]{1,0:T(8,128)(2,1)} custom-call(s32[1]{0:T(128)} %bitcast.first_ref, s32[512,1]{1,0:T(8,128)S(1)} %copy-done.10, bf16[512,1792]{1,0:T(8,128)(2,1)S(1)} %copy-done.12, f32[512,28]{1,0:T(8,128)S(1)} %copy-done.8, bf16[512,64]{1,0:T(8,128)(2,1)S(1)} %constant_dynamic-slice_fusion.1.b_ref, ...), custom_call_target="tpu_custom_call" | custom-call | flops 5000000000 | bytes 6000000 | tf_op jit(solution)/shard_map/pallas_call | solution.py:359
  140.9 13.4 %all-to-all-done.3.a_ref = bf16[32,224,128]{2,1,0:T(8,128)(2,1)} async-done(((bf16[32,224,128]{2,1,0:T(8,128)(2,1)}), bf16[32,224,128]{2,1,0:T(8,128)(2,1)}, u32[]{:S(2)}, u32[]{:S(2)}) %all-to-all-start.3) | async-done | bytes 1835040 | tf_op jit(solution)/shard_map/all_to_all | solution.py:389
  154.3 2.7 %shard_map.120 = bf16[128,7168]{1,0:T(8,128)(2,1)} custom-call(bf16[32,224,128]{2,1,0:T(8,128)(2,1)} %all-to-all-done.3.a_ref), custom_call_target="tpu_custom_call" | custom-call | bytes 3670016 | tf_op jit(solution)/shard_map/pallas_call | solution.py:101
  (62 shorter events, 4.5 us)
Async XLA Ops:
  0.6 16.6 %copy-start = (bf16[512,128]{1,0:T(8,128)(2,1)S(1)}, bf16[512,128]{1,0:T(8,128)(2,1)}, u32[]{:S(2)}) copy-start(bf16[512,128]{1,0:T(8,128)(2,1)} %param.15) | copy-start | bytes 393220
  3.2 32.9 %all-to-all-start = ((bf16[32,224,128]{2,1,0:T(8,128)(2,1)}), bf16[32,224,128]{2,1,0:T(8,128)(2,1)S(1)}, u32[]{:S(2)}, u32[]{:S(2)}) async-start(bf16[32,224,128]{2,1,0:T(8,128)(2,1)} %shard_map.116), calls=%async_computation | async-start | bytes 3670016 | tf_op jit(solution)/shard_map/all_to_all | solution.py:389
  10.6 1.5 copy-start.4
  12.1 3.3 %copy-start.19 = (s32[64]{0:T(128)S(1)}, s32[64]{0:T(128)}, u32[]{:S(2)}) copy-start(s32[64]{0:T(128)} %param.19) | copy-start | bytes 772
  12.1 4.6 %copy-start.17 = (f32[512,28]{0,1:T(8,128)S(1)}, f32[512,28]{0,1:T(8,128)}, u32[]{:S(2)}) copy-start(f32[512,28]{0,1:T(8,128)} %param.14) | copy-start | bytes 172036
  14.1 1.2 copy-start.1
  15.4 2.3 %copy-start.15 = (f32[28]{0:T(128)S(1)}, f32[28]{0:T(128)}, u32[]{:S(2)}) copy-start(f32[28]{0:T(128)} %param.17) | copy-start | bytes 340
  16.8 8.1 %copy-start.7 = (f32[512,28]{1,0:T(8,128)}, f32[512,28]{1,0:T(8,128)S(1)}, u32[]{:S(2)}) copy-start(f32[512,28]{1,0:T(8,128)S(1)} %copy.22.step_ref) | copy-start | bytes 172036
  17.7 1.0 copy-start.9
  18.7 1.5 copy-start.11
  24.9 53.1 %copy-start.18 = (s32[4096]{0:T(1024)}, s32[4096]{0:T(1024)S(1)}, u32[]{:S(2)}) copy-start(s32[4096]{0:T(1024)S(1)} %broadcast_subtract_fusion) | copy-start | bytes 49156
  36.2 30.3 %all-to-all-start.2 = ((bf16[32,224,128]{2,1,0:T(8,128)(2,1)}), bf16[32,224,128]{2,1,0:T(8,128)(2,1)}, u32[]{:S(2)}, u32[]{:S(2)}) async-start(bf16[32,224,128]{2,1,0:T(8,128)(2,1)} %copy-done.1), calls=%async_computation.2 | async-start | bytes 3670016 | tf_op jit(solution)/shard_map/all_to_all | solution.py:389
  41.0 19.4 %collective-permute-start = (bf16[12,224,128]{2,1,0:T(8,128)(2,1)S(1)}, bf16[12,224,128]{2,1,0:T(8,128)(2,1)S(1)}, u32[]{:S(2)}, u32[]{:S(2)}) collective-permute-start(bf16[12,224,128]{2,1,0:T(8,128)(2,1)S(1)} %slice.24), channel_id=1, source_target_pairs={{0,32},{32,64},{64,96},{1,33},{33,65},{65,97},{2,34},{34,66},{66,9... | collective-permute-start | bytes 2064392 | tf_op jit(solution)/shard_map/ppermute | solution.py:419
  44.5 1.5 copy-start.5
  48.1 1.2 copy-start.2
  50.4 1.3 copy-start.3
  60.8 5.8 %copy-start.6 = (bf16[1536,224]{1,0:T(8,128)(2,1)}, bf16[1536,224]{1,0:T(8,128)(2,1)S(1)}, u32[]{:S(2)}) copy-start(bf16[1536,224]{1,0:T(8,128)(2,1)S(1)} %shard_map.118.halo_k) | copy-start | bytes 2064388
  66.5 34.5 %all-to-all-start.1 = ((bf16[32,224,128]{2,1,0:T(8,128)(2,1)}), bf16[32,224,128]{2,1,0:T(8,128)(2,1)}, u32[]{:S(2)}, u32[]{:S(2)}) async-start(bf16[32,224,128]{2,1,0:T(8,128)(2,1)} %copy-done.2), calls=%async_computation.1 | async-start | bytes 3670016 | tf_op jit(solution)/shard_map/all_to_all | solution.py:389
  71.3 28.9 %collective-permute-start.2 = (f32[72,1792]{1,0:T(8,128)S(1)}, f32[72,1792]{1,0:T(8,128)S(1)}, u32[]{:S(2)}, u32[]{:S(2)}) collective-permute-start(f32[72,1792]{1,0:T(8,128)S(1)} %shard_map.114), channel_id=1, source_target_pairs={{0,4},{4,8},{8,12},{12,16},{16,20},{20,24},{24,28},{28,32},{32,36}... | collective-permute-start | bytes 1548296 | tf_op jit(solution)/shard_map/ppermute | solution.py:417
  74.4 26.5 %collective-permute-start.1 = (bf16[12,224,128]{2,1,0:T(8,128)(2,1)S(1)}, bf16[12,224,128]{2,1,0:T(8,128)(2,1)S(1)}, u32[]{:S(2)}, u32[]{:S(2)}) collective-permute-start(bf16[12,224,128]{2,1,0:T(8,128)(2,1)S(1)} %slice.25), channel_id=1, source_target_pairs={{0,32},{32,64},{64,96},{1,33},{33,65},{65,97},{2,34},{34,66},{66,9... | collective-permute-start | bytes 2064392 | tf_op jit(solution)/shard_map/ppermute | solution.py:425
  101.0 2.6 %copy-start.21 = (bf16[12,224,128]{2,1,0:T(8,128)(2,1)}, bf16[12,224,128]{2,1,0:T(8,128)(2,1)S(1)}, u32[]{:S(2)}) copy-start(bf16[12,224,128]{2,1,0:T(8,128)(2,1)S(1)} %collective-permute-done.1.halo_v) | copy-start | bytes 2064388
  101.0 18.1 %collective-permute-start.3 = (f32[64,1792]{1,0:T(8,128)}, f32[64,1792]{1,0:T(8,128)S(1)}, u32[]{:S(2)}, u32[]{:S(2)}) collective-permute-start(f32[64,1792]{1,0:T(8,128)} %fusion), channel_id=1, source_target_pairs={{0,8},{4,12},{8,16},{12,20},{16,24},{20,28},{24,32},{28,36},{32,40... | collective-permute-start | bytes 1376264 | tf_op jit(solution)/shard_map/ppermute | solution.py:428
  119.0 9.7 %copy-start.20 = (f32[28]{0:T(128)S(1)}, f32[28]{0:T(128)}, u32[]{:S(2)}) copy-start(f32[28]{0:T(128)} %param.18) | copy-start | bytes 340
  119.1 9.8 %copy-start.16 = (bf16[512,128]{1,0:T(8,128)(2,1)S(1)}, bf16[512,128]{1,0:T(8,128)(2,1)}, u32[]{:S(2)}) copy-start(bf16[512,128]{1,0:T(8,128)(2,1)} %param.16) | copy-start | bytes 393220
  119.1 9.9 %copy-start.8 = (f32[512,28]{1,0:T(8,128)S(1)}, f32[512,28]{1,0:T(8,128)}, u32[]{:S(2)}) copy-start(f32[512,28]{1,0:T(8,128)} %copy-done.7) | copy-start | bytes 172036
  119.1 9.9 %copy-start.12 = (bf16[512,1792]{1,0:T(8,128)(2,1)S(1)}, bf16[512,1792]{1,0:T(8,128)(2,1)}, u32[]{:S(2)}) copy-start(bf16[512,1792]{1,0:T(8,128)(2,1)} %x_ref.3) | copy-start | bytes 5505028
  119.1 0.8 copy-start.13
  119.9 34.4 %all-to-all-start.3 = ((bf16[32,224,128]{2,1,0:T(8,128)(2,1)}), bf16[32,224,128]{2,1,0:T(8,128)(2,1)}, u32[]{:S(2)}, u32[]{:S(2)}) async-start(bf16[32,224,128]{2,1,0:T(8,128)(2,1)} %shard_map.119), calls=%async_computation.3 | async-start | bytes 3670016 | tf_op jit(solution)/shard_map/all_to_all | solution.py:389
  129.0 1.0 copy-start.10
  130.0 1.0 copy-start.14

commit v2 on v1

--- a/solution.py
+++ b/solution.py
@@ -104,7 +104,7 @@
         in_specs=[pl.BlockSpec((step, ATT_HD, BLOCK), lambda i: (i, 0, 0))],
         out_specs=pl.BlockSpec((BLOCK, step * ATT_HD), lambda i: (0, i)),
         out_shape=jax.ShapeDtypeStruct((BLOCK, heads * ATT_HD), BF16),
-        compiler_params=compiler_params(),
+        compiler_params=compiler_params(16),
         cost_estimate=pl.CostEstimate(flops=0, bytes_accessed=4 * BLOCK * heads * ATT_HD, transcendentals=0),
     )(blocks)
 
@@ -182,33 +182,57 @@
         def attend_over(reach):
             first = 2 * p + halo // per + 1 - reach
             rows = pl.multiple_of(first * TILE, TILE)
-            for half in range(2):
-                j = 2 * p + half
-                count = reach + half
-                q_t = jnp.concatenate([q_own[per * j + i] for i in range(per)], axis=1)
-                start = starts_ref[j]
-                scores = []
-                for i in range(count):
-                    s = dot(k_rows[pl.ds(rows + i * TILE, TILE), :], q_t)
-                    kept = down >= start - (j - count + 1 + i) * TILE
-                    if i == count - 1:
-                        kept = jnp.logical_and(kept, causal)
-                    scores.append(jnp.where(kept, s, -1e30))
-                top = scores[0]
-                for s in scores[1:]:
-                    top = jnp.maximum(top, s)
-                top = jnp.max(top, axis=0, keepdims=True)
-                total = jnp.zeros((TILE, TILE), F32)
-                mixed = jnp.zeros((ATT_HD, TILE), F32)
-                for i in range(count):
-                    weights = jnp.exp2((scores[i] - top) * factor)
-                    total = total + weights
-                    v_t = jnp.concatenate([v_cols[first * per + i * per + b] for b in range(per)], axis=1)
-                    mixed = mixed + dot(v_t, weights.astype(BF16))
-                total = jnp.sum(total, axis=0, keepdims=True)
-                out = (mixed * (1.0 / total)).astype(BF16)
+            starts = [starts_ref[2 * p + half] for half in range(2)]
+            queries = [
+                jnp.concatenate([q_own[per * (2 * p + half) + i] for i in range(per)], axis=1) for half in range(2)
+            ]
+            counts = [reach, reach + 1]
+
+            def score(half, i):
+                s = dot(k_rows[pl.ds(rows + i * TILE, TILE), :], queries[half])
+                kept = down >= starts[half] - (2 * p + half - counts[half] + 1 + i) * TILE
+                if i == counts[half] - 1:
+                    kept = jnp.logical_and(kept, causal)
+                return jnp.where(kept, s, -1e30)
+
+            def peak(scores):
+                tops = [jnp.max(jnp.reshape(s, (TILE // 8, 8, TILE)), axis=0) for s in scores]
+                return jnp.max(functools.reduce(jnp.maximum, tops), axis=0, keepdims=True)
+
+            def values(i):
+                return jnp.concatenate([v_cols[first * per + i * per + b] for b in range(per)], axis=1)
+
+            def put(half, mixed, total):
+                out = (mixed * (1.0 / jnp.sum(total, axis=0, keepdims=True))).astype(BF16)
                 for b in range(per):
-                    o_own[per * j + b] = out[:, b * BLOCK : (b + 1) * BLOCK]
+                    o_own[per * (2 * p + half) + b] = out[:, b * BLOCK : (b + 1) * BLOCK]
+
+            def weigh(s, top, total):
+                weights = jnp.exp2((s - top) * factor)
+                return weights.astype(BF16), total + jnp.sum(jnp.reshape(weights, (TILE // 8, 8, TILE)), axis=0)
+
+            total = [jnp.zeros((8, TILE), F32)] * 2
+            mixed = [jnp.zeros((ATT_HD, TILE), F32)] * 2
+            near_scores = [score(0, i) for i in range(counts[0])]
+            near_top = peak(near_scores)
+            near_weights, scores = [], []
+            for i in range(counts[1]):
+                scores.append(score(1, i))
+                if i < counts[0]:
+                    weights, total[0] = weigh(near_scores[i], near_top, total[0])
+                    near_weights.append(weights)
+            top = peak(scores)
+            last = None
+            for i in range(counts[1]):
+                if i < counts[0]:
+                    mixed[0] = mixed[0] + dot(values(i), near_weights[i])
+                weights, total[1] = weigh(scores[i], top, total[1])
+                if last is not None:
+                    mixed[1] = mixed[1] + dot(values(i - 1), last)
+                last = weights
+            put(0, mixed[0], total[0])
+            mixed[1] = mixed[1] + dot(values(counts[1] - 1), last)
+            put(1, mixed[1], total[1])
 
         for count in range(1, most + 1):
             pl.when(reach == count)(functools.partial(attend_over, count))
@@ -249,7 +273,7 @@
             pltpu.SemaphoreType.DMA((tiles // 2,)),
         ],
         compiler_params=compiler_params(60),
-        cost_estimate=pl.CostEstimate(flops=4_000_000_000, bytes_accessed=8_000_000, transcendentals=4_000_000),
+        cost_estimate=pl.CostEstimate(flops=1_000_000, bytes_accessed=1_000_000, transcendentals=0),
     )(reach, by_tile, q_blocks, own_rows, own_v, halo_rows, halo_v)
 
 
@@ -411,19 +435,20 @@
     c_group = lax.dynamic_slice_in_dim(out_proj_c, group * width, width, 1)
     state, finish = scan_parts(ssm_input, step_size, b_group, c_group, decay_rate, skip_gain, start, first)
     starts = doc_start(plane_first + jnp.arange(plane_tokens), doc_lengths) - plane_first
-    v_blocks, state, starts = together((turn([values_in], 16), state, starts))
+    values_in, state = together((values_in, state))
+    near = lax.ppermute(state, CTX, [(i, i + 1) for i in range(devices - 1)])
+    v_blocks, near, starts = together((turn([values_in], 16), near, starts))
 
     v = exchange(v_blocks)
-    near = lax.ppermute(state, CTX, [(i, i + 1) for i in range(devices - 1)])
-    two = state[:width] + state[width : width + 1] * near[:width]
     halo_k = lax.ppermute(k[-halo_blocks:], "z", to_next)
     own_rows = key_rows(k)
     halo_rows = key_rows(halo_k)
-    q_blocks, own_rows, halo_rows = together((turn([queries], 16), own_rows, halo_rows))
+    two = state[:width] + state[width : width + 1] * near[:width]
+    q_blocks, own_rows, halo_rows, two = together((turn([queries], 16), own_rows, halo_rows, two))
 
     q = exchange(q_blocks)
     halo_v = lax.ppermute(v[-halo_blocks:], "z", to_next)
-    q, halo_v, two = together((q, halo_v, two))
+    q, halo_v = together((q, halo_v))
 
     far = lax.ppermute(two, CTX, [(i, i + 2) for i in range(devices - 2)])
     o_blocks, far = together((attend(q, own_rows, v, halo_rows, halo_v, starts), far))

time: 157 us -> 148 us (0.943)
  waiting for transfers between devices: 61 us -> 56.9 us
  local copies, waits for them, and re-layouts: 15.3 us -> 12.6 us
  Pallas kernels: 40.8 us -> 39.1 us
    ppermute x1, waiting for transfers between devices: 0.01 us -> 11.2 us  [local(): halo_v = lax.ppermute(v[-halo_blocks:], 'z', to_next)]
    ppermute x1, waiting for transfers between devices: 21.9 us -> 13.3 us  [local(): near = lax.ppermute(state, CTX, [(i, i + 1) for i in range(devices - 1)])]
    all_to_all x4, waiting for transfers between devices: 30.5 us -> 24.5 us  [exchange(): lax.all_to_all(blocks, PLANE, split_axis=0, concat_axis=0, tiled=True)]
    all_to_all x4, starting transfers between devices: 25.6 us -> 22.8 us  [exchange(): lax.all_to_all(blocks, PLANE, split_axis=0, concat_axis=0, tiled=True)]
    unnamed x45 -> x41, local copies, waits for them, and re-layouts: 12.1 us -> 9.39 us
    pallas_call x1, Pallas kernels: 15.4 us -> 13 us  [attend(): pl.pallas_call(functools.partial(attend_kernel, most), in_specs=[pl.Block...]
    ppermute x1, starting transfers between devices: 2.1 us -> 3.75 us  [local(): far = lax.ppermute(two, CTX, [(i, i + 2) for i in range(devices - 2)])]
  transfers between devices with their start and end apart: 8 -> 8, of which waited for: 5 -> 6; matrix products, arithmetic and copies ran while one was open for 3% -> 4% of each run, Pallas kernels for 23% -> 23%
where the time goes in v2:
time: 148 us; the launch traced here: 147 us
  waiting for transfers between devices  56.9 us (38%)
  Pallas kernels  39.1 us (26%)
  starting transfers between devices  35.8 us (24%)
  local copies, waits for them, and re-layouts  12.6 us (9%)
  other arithmetic  2.06 us (1%)
    all_to_all x4, waiting for transfers between devices, exchange(): lax.all_to_all(blocks, PLANE, split_axis=0, concat_axis=0, tiled=True)  24.5 us
    all_to_all x4, starting transfers between devices, exchange(): lax.all_to_all(blocks, PLANE, split_axis=0, concat_axis=0, tiled=True)  22.8 us
    ppermute x1, waiting for transfers between devices, local(): near = lax.ppermute(state, CTX, [(i, i + 1) for i in range(devices - 1)])  13.3 us
    pallas_call x1, Pallas kernels, attend(): pl.pallas_call(functools.partial(attend_kernel, most), in_specs=[pl.Block...  13 us
    ppermute x1, waiting for transfers between devices, local(): halo_v = lax.ppermute(v[-halo_blocks:], 'z', to_next)  11.2 us
    pallas_call x1, Pallas kernels, finish(): pl.pallas_call(scan_kernel, grid=(width // chunk,), in_specs=[smem, whole...  10.6 us
    unnamed x41, local copies, waits for them, and re-layouts  9.39 us
    ppermute x1, waiting for transfers between devices, local(): halo_k = lax.ppermute(k[-halo_blocks:], 'z', to_next)  7.84 us
  transfers between devices with their start and end apart: 8, of which 6 were waited for; matrix products, arithmetic and copies ran while one was open for 4% of the time, Pallas kernels for 23%

profile of v2, /device:TPU:64, one launch (start us, length us, event | category | flops | bytes accessed | tf_op | source)
XLA Modules:
  0.0 147.5 jit_solution(17410527214157273487)
XLA Ops:
  0.6 2.6 %shard_map.116 = bf16[32,224,128]{2,1,0:T(8,128)(2,1)} custom-call(bf16[128,7168]{1,0:T(8,128)(2,1)} %refs_0_.4), custom_call_target="tpu_custom_call" | custom-call | bytes 3670016 | tf_op jit(solution)/shard_map/pallas_call | solution.py:77
  3.3 7.5 %all-to-all-start = ((bf16[32,224,128]{2,1,0:T(8,128)(2,1)}), bf16[32,224,128]{2,1,0:T(8,128)(2,1)S(1)}, u32[]{:S(2)}, u32[]{:S(2)}) async-start(bf16[32,224,128]{2,1,0:T(8,128)(2,1)} %shard_map.116), calls=%async_computation | async-start | bytes 3670016 | tf_op jit(solution)/shard_map/all_to_all | solution.py:413
  11.2 0.9 copy.21.start_ref
  13.4 0.9 copy-done.9
  14.3 1.5 %copy-done.11 = bf16[512,1792]{1,0:T(8,128)(2,1)S(1)} copy-done((bf16[512,1792]{1,0:T(8,128)(2,1)S(1)}, bf16[512,1792]{1,0:T(8,128)(2,1)}, u32[]{:S(2)}) %copy-start.11) | copy-done | bytes 1835032
  15.8 4.7 %shard_map.113 = f32[72,1792]{1,0:T(8,128)S(1)} custom-call(s32[1]{0:T(128)} %bitcast.first_ref, s32[512,1]{1,0:T(8,128)S(1)} %copy-done.9, bf16[512,1792]{1,0:T(8,128)(2,1)S(1)} %copy-done.11, f32[512,28]{1,0:T(8,128)S(1)} %copy.22.step_ref, bf16[512,64]{1,0:T(8,128)(2,1)S(1)} %constant_dynamic-slice_fusion.1.b_ref, f32[1,28]{1,0:T(1,128)S(1)} %bitcast.5, ...), custom_call_target="tpu_custom_call" | custom-call | flops 2000000000 | bytes 3000000 | tf_op jit(solution)/shard_map/pallas_call | solution.py:368
  20.6 2.2 %collective-permute-start = (f32[72,1792]{1,0:T(8,128)S(1)}, f32[72,1792]{1,0:T(8,128)S(1)}, u32[]{:S(2)}, u32[]{:S(2)}) collective-permute-start(f32[72,1792]{1,0:T(8,128)S(1)} %shard_map.113), channel_id=1, source_target_pairs={{0,4},{4,8},{8,12},{12,16},{16,20},{20,24},{24,28},{28,32},{32,36}... | collective-permute-start | bytes 1548296 | tf_op jit(solution)/shard_map/ppermute | solution.py:439
  22.8 2.0 %shard_map.114 = bf16[32,224,128]{2,1,0:T(8,128)(2,1)S(1)} custom-call(bf16[128,7168]{1,0:T(8,128)(2,1)S(1)} %copy-done.5), custom_call_target="tpu_custom_call" | custom-call | bytes 3670016 | tf_op jit(solution)/shard_map/pallas_call | solution.py:77
  24.8 1.2 copy-done.2
  26.3 13.3 %collective-permute-done.near_ref = f32[72,1792]{1,0:T(8,128)S(1)} collective-permute-done((f32[72,1792]{1,0:T(8,128)S(1)}, f32[72,1792]{1,0:T(8,128)S(1)}, u32[]{:S(2)}, u32[]{:S(2)}) %collective-permute-start) | collective-permute-done | bytes 516128 | tf_op jit(solution)/shard_map/ppermute | solution.py:439
  39.6 5.7 %all-to-all-start.2 = ((bf16[32,224,128]{2,1,0:T(8,128)(2,1)}), bf16[32,224,128]{2,1,0:T(8,128)(2,1)}, u32[]{:S(2)}, u32[]{:S(2)}) async-start(bf16[32,224,128]{2,1,0:T(8,128)(2,1)} %copy-done.2), calls=%async_computation.2 | async-start | bytes 3670016 | tf_op jit(solution)/shard_map/all_to_all | solution.py:413
  45.4 3.5 %collective-permute-start.1 = (bf16[12,224,128]{2,1,0:T(8,128)(2,1)S(1)}, bf16[12,224,128]{2,1,0:T(8,128)(2,1)S(1)}, u32[]{:S(2)}, u32[]{:S(2)}) collective-permute-start(bf16[12,224,128]{2,1,0:T(8,128)(2,1)S(1)} %slice.24), channel_id=1, source_target_pairs={{0,32},{32,64},{64,96},{1,33},{33,65},{65,97},{2,34},{34,66},{66,9... | collective-permute-start | bytes 2064392 | tf_op jit(solution)/shard_map/ppermute | solution.py:443
  48.9 1.5 %copy-done.6 = bf16[128,7168]{1,0:T(8,128)(2,1)S(1)} copy-done((bf16[128,7168]{1,0:T(8,128)(2,1)S(1)}, bf16[128,7168]{1,0:T(8,128)(2,1)}, u32[]{:S(2)}) %copy-start.6) | copy-done | bytes 1835032
  50.4 2.0 %shard_map.115 = bf16[32,224,128]{2,1,0:T(8,128)(2,1)S(1)} custom-call(bf16[128,7168]{1,0:T(8,128)(2,1)S(1)} %copy-done.6), custom_call_target="tpu_custom_call" | custom-call | bytes 3670016 | tf_op jit(solution)/shard_map/pallas_call | solution.py:77
  52.5 1.2 copy-done.3
  53.7 0.9 multiply_add_fusion
  54.6 1.0 shard_map.117.own_k
  55.7 1.3 copy-done.1
  57.0 7.8 %collective-permute-done.1.k_ref = bf16[12,224,128]{2,1,0:T(8,128)(2,1)S(1)} collective-permute-done((bf16[12,224,128]{2,1,0:T(8,128)(2,1)S(1)}, bf16[12,224,128]{2,1,0:T(8,128)(2,1)S(1)}, u32[]{:S(2)}, u32[]{:S(2)}) %collective-permute-start.1) | collective-permute-done | bytes 688160 | tf_op jit(solution)/shard_map/ppermute | solution.py:443
  65.2 5.7 %all-to-all-done.2.own_v = bf16[32,224,128]{2,1,0:T(8,128)(2,1)} async-done(((bf16[32,224,128]{2,1,0:T(8,128)(2,1)}), bf16[32,224,128]{2,1,0:T(8,128)(2,1)}, u32[]{:S(2)}, u32[]{:S(2)}) %all-to-all-start.2) | async-done | bytes 1835040 | tf_op jit(solution)/shard_map/all_to_all | solution.py:413
  70.9 4.7 %all-to-all-start.1 = ((bf16[32,224,128]{2,1,0:T(8,128)(2,1)}), bf16[32,224,128]{2,1,0:T(8,128)(2,1)}, u32[]{:S(2)}, u32[]{:S(2)}) async-start(bf16[32,224,128]{2,1,0:T(8,128)(2,1)} %copy-done.3), calls=%async_computation.1 | async-start | bytes 3670016 | tf_op jit(solution)/shard_map/all_to_all | solution.py:413
  75.7 1.1 slice.25
  76.8 3.5 %collective-permute-start.2 = (bf16[12,224,128]{2,1,0:T(8,128)(2,1)S(1)}, bf16[12,224,128]{2,1,0:T(8,128)(2,1)S(1)}, u32[]{:S(2)}, u32[]{:S(2)}) collective-permute-start(bf16[12,224,128]{2,1,0:T(8,128)(2,1)S(1)} %slice.25), channel_id=1, source_target_pairs={{0,32},{32,64},{64,96},{1,33},{33,65},{65,97},{2,34},{34,66},{66,9... | collective-permute-start | bytes 2064392 | tf_op jit(solution)/shard_map/ppermute | solution.py:450
  80.4 3.8 %collective-permute-start.3 = (f32[64,1792]{1,0:T(8,128)}, f32[64,1792]{1,0:T(8,128)}, u32[]{:S(2)}, u32[]{:S(2)}) collective-permute-start(f32[64,1792]{1,0:T(8,128)} %multiply_add_fusion), channel_id=1, source_target_pairs={{0,8},{4,12},{8,16},{12,20},{16,24},{20,28},{24,32},{28,36},{32,40... | collective-permute-start | bytes 1376264 | tf_op jit(solution)/shard_map/ppermute | solution.py:453
  84.9 11.2 %collective-permute-done.2.halo_v = bf16[12,224,128]{2,1,0:T(8,128)(2,1)S(1)} collective-permute-done((bf16[12,224,128]{2,1,0:T(8,128)(2,1)S(1)}, bf16[12,224,128]{2,1,0:T(8,128)(2,1)S(1)}, u32[]{:S(2)}, u32[]{:S(2)}) %collective-permute-start.2) | collective-permute-done | bytes 688160 | tf_op jit(solution)/shard_map/ppermute | solution.py:450
  96.2 5.1 %all-to-all-done.1.q_ref = bf16[32,224,128]{2,1,0:T(8,128)(2,1)} async-done(((bf16[32,224,128]{2,1,0:T(8,128)(2,1)}), bf16[32,224,128]{2,1,0:T(8,128)(2,1)}, u32[]{:S(2)}, u32[]{:S(2)}) %all-to-all-start.1) | async-done | bytes 1835040 | tf_op jit(solution)/shard_map/all_to_all | solution.py:413
  101.2 13.0 %shard_map.119 = bf16[32,224,128]{2,1,0:T(8,128)(2,1)} custom-call(s32[8]{0:T(128)} %subtract_add_fusion.reach_ref, s32[16,1,256]{2,1,0:T(1,128)} %bitcast.8, bf16[32,224,128]{2,1,0:T(8,128)(2,1)} %all-to-all-done.1.q_ref, bf16[4096,224]{1,0:T(8,128)(2,1)} %copy-done.1, bf16[32,224,128]{2,1,0:T(8,128)(2,1)} %all-to-all-done.2.own_v, ...), custom_call_target="tpu_custom_call" | custom-call | flops 1000000 | bytes 1000000 | tf_op jit(solution)/shard_map/pallas_call | solution.py:261
  114.3 4.9 %all-to-all-start.3 = ((bf16[32,224,128]{2,1,0:T(8,128)(2,1)}), bf16[32,224,128]{2,1,0:T(8,128)(2,1)}, u32[]{:S(2)}, u32[]{:S(2)}) async-start(bf16[32,224,128]{2,1,0:T(8,128)(2,1)} %shard_map.119), calls=%async_computation.3 | async-start | bytes 3670016 | tf_op jit(solution)/shard_map/all_to_all | solution.py:413
  119.5 0.9 copy-done.10
  120.5 10.6 %shard_map.121 = bf16[512,1792]{1,0:T(8,128)(2,1)} custom-call(s32[1]{0:T(128)} %bitcast.first_ref, s32[512,1]{1,0:T(8,128)S(1)} %copy-done.10, bf16[512,1792]{1,0:T(8,128)(2,1)S(1)} %copy-done.12, f32[512,28]{1,0:T(8,128)S(1)} %copy-done.8, bf16[512,64]{1,0:T(8,128)(2,1)S(1)} %constant_dynamic-slice_fusion.1.b_ref, ...), custom_call_target="tpu_custom_call" | custom-call | flops 5000000000 | bytes 6000000 | tf_op jit(solution)/shard_map/pallas_call | solution.py:383
  131.1 13.7 %all-to-all-done.3.a_ref = bf16[32,224,128]{2,1,0:T(8,128)(2,1)} async-done(((bf16[32,224,128]{2,1,0:T(8,128)(2,1)}), bf16[32,224,128]{2,1,0:T(8,128)(2,1)}, u32[]{:S(2)}, u32[]{:S(2)}) %all-to-all-start.3) | async-done | bytes 1835040 | tf_op jit(solution)/shard_map/all_to_all | solution.py:413
  144.8 2.7 %shard_map.120 = bf16[128,7168]{1,0:T(8,128)(2,1)} custom-call(bf16[32,224,128]{2,1,0:T(8,128)(2,1)} %all-to-all-done.3.a_ref), custom_call_target="tpu_custom_call" | custom-call | bytes 3670016 | tf_op jit(solution)/shard_map/pallas_call | solution.py:101
  (58 shorter events, 3.5 us)
Async XLA Ops:
  0.6 12.1 %copy-start = (bf16[512,128]{1,0:T(8,128)(2,1)S(1)}, bf16[512,128]{1,0:T(8,128)(2,1)}, u32[]{:S(2)}) copy-start(bf16[512,128]{1,0:T(8,128)(2,1)} %param.15) | copy-start | bytes 393220
  3.2 7.5 %copy-start.18 = (s32[64]{0:T(128)S(1)}, s32[64]{0:T(128)}, u32[]{:S(2)}) copy-start(s32[64]{0:T(128)} %param.19) | copy-start | bytes 772
  3.3 9.3 %copy-start.17 = (f32[512,28]{0,1:T(8,128)S(1)}, f32[512,28]{0,1:T(8,128)}, u32[]{:S(2)}) copy-start(f32[512,28]{0,1:T(8,128)} %param.14) | copy-start | bytes 172036
  3.3 36.4 %all-to-all-start = ((bf16[32,224,128]{2,1,0:T(8,128)(2,1)}), bf16[32,224,128]{2,1,0:T(8,128)(2,1)S(1)}, u32[]{:S(2)}, u32[]{:S(2)}) async-start(bf16[32,224,128]{2,1,0:T(8,128)(2,1)} %shard_map.116), calls=%async_computation | async-start | bytes 3670016 | tf_op jit(solution)/shard_map/all_to_all | solution.py:413
  10.7 2.6 %copy-start.13 = (f32[28]{0:T(128)S(1)}, f32[28]{0:T(128)}, u32[]{:S(2)}) copy-start(f32[28]{0:T(128)} %param.17) | copy-start | bytes 340
  12.7 0.7 copy-start.7
  13.4 1.0 copy-start.9
  14.3 1.5 %copy-start.11 = (bf16[512,1792]{1,0:T(8,128)(2,1)S(1)}, bf16[512,1792]{1,0:T(8,128)(2,1)}, u32[]{:S(2)}) copy-start(bf16[512,1792]{1,0:T(8,128)(2,1)} %x_ref.3) | copy-start | bytes 5505028
  15.8 6.9 %copy-start.5 = (bf16[128,7168]{1,0:T(8,128)(2,1)S(1)}, bf16[128,7168]{1,0:T(8,128)(2,1)}, u32[]{:S(2)}) copy-start(bf16[128,7168]{1,0:T(8,128)(2,1)} %refs_0_.2) | copy-start | bytes 5505028
  20.6 19.0 %collective-permute-start = (f32[72,1792]{1,0:T(8,128)S(1)}, f32[72,1792]{1,0:T(8,128)S(1)}, u32[]{:S(2)}, u32[]{:S(2)}) collective-permute-start(f32[72,1792]{1,0:T(8,128)S(1)} %shard_map.113), channel_id=1, source_target_pairs={{0,4},{4,8},{8,12},{12,16},{16,20},{20,24},{24,28},{28,32},{32,36}... | collective-permute-start | bytes 1548296 | tf_op jit(solution)/shard_map/ppermute | solution.py:439
  24.8 1.2 copy-start.2
  26.3 57.8 %copy-start.16 = (s32[4096]{0:T(1024)}, s32[4096]{0:T(1024)S(1)}, u32[]{:S(2)}) copy-start(s32[4096]{0:T(1024)S(1)} %broadcast_subtract_fusion) | copy-start | bytes 49156
  39.6 31.3 %all-to-all-start.2 = ((bf16[32,224,128]{2,1,0:T(8,128)(2,1)}), bf16[32,224,128]{2,1,0:T(8,128)(2,1)}, u32[]{:S(2)}, u32[]{:S(2)}) async-start(bf16[32,224,128]{2,1,0:T(8,128)(2,1)} %copy-done.2), calls=%async_computation.2 | async-start | bytes 3670016 | tf_op jit(solution)/shard_map/all_to_all | solution.py:413
  45.4 19.4 %collective-permute-start.1 = (bf16[12,224,128]{2,1,0:T(8,128)(2,1)S(1)}, bf16[12,224,128]{2,1,0:T(8,128)(2,1)S(1)}, u32[]{:S(2)}, u32[]{:S(2)}) collective-permute-start(bf16[12,224,128]{2,1,0:T(8,128)(2,1)S(1)} %slice.24), channel_id=1, source_target_pairs={{0,32},{32,64},{64,96},{1,33},{33,65},{65,97},{2,34},{34,66},{66,9... | collective-permute-start | bytes 2064392 | tf_op jit(solution)/shard_map/ppermute | solution.py:443
  48.9 1.5 %copy-start.6 = (bf16[128,7168]{1,0:T(8,128)(2,1)S(1)}, bf16[128,7168]{1,0:T(8,128)(2,1)}, u32[]{:S(2)}) copy-start(bf16[128,7168]{1,0:T(8,128)(2,1)} %refs_0_.3) | copy-start | bytes 5505028
  52.5 1.2 copy-start.3
  55.6 1.3 copy-start.1
  65.2 5.7 %copy-start.4 = (bf16[1536,224]{1,0:T(8,128)(2,1)}, bf16[1536,224]{1,0:T(8,128)(2,1)S(1)}, u32[]{:S(2)}) copy-start(bf16[1536,224]{1,0:T(8,128)(2,1)S(1)} %shard_map.118.halo_k) | copy-start | bytes 2064388
  70.9 30.3 %all-to-all-start.1 = ((bf16[32,224,128]{2,1,0:T(8,128)(2,1)}), bf16[32,224,128]{2,1,0:T(8,128)(2,1)}, u32[]{:S(2)}, u32[]{:S(2)}) async-start(bf16[32,224,128]{2,1,0:T(8,128)(2,1)} %copy-done.3), calls=%async_computation.1 | async-start | bytes 3670016 | tf_op jit(solution)/shard_map/all_to_all | solution.py:413
  76.8 19.4 %collective-permute-start.2 = (bf16[12,224,128]{2,1,0:T(8,128)(2,1)S(1)}, bf16[12,224,128]{2,1,0:T(8,128)(2,1)S(1)}, u32[]{:S(2)}, u32[]{:S(2)}) collective-permute-start(bf16[12,224,128]{2,1,0:T(8,128)(2,1)S(1)} %slice.25), channel_id=1, source_target_pairs={{0,32},{32,64},{64,96},{1,33},{33,65},{65,97},{2,34},{34,66},{66,9... | collective-permute-start | bytes 2064392 | tf_op jit(solution)/shard_map/ppermute | solution.py:450
  80.4 34.0 %collective-permute-start.3 = (f32[64,1792]{1,0:T(8,128)}, f32[64,1792]{1,0:T(8,128)}, u32[]{:S(2)}, u32[]{:S(2)}) collective-permute-start(f32[64,1792]{1,0:T(8,128)} %multiply_add_fusion), channel_id=1, source_target_pairs={{0,8},{4,12},{8,16},{12,20},{16,24},{20,28},{24,32},{28,36},{32,40... | collective-permute-start | bytes 1376264 | tf_op jit(solution)/shard_map/ppermute | solution.py:453
  96.2 5.1 %copy-start.14 = (bf16[12,224,128]{2,1,0:T(8,128)(2,1)}, bf16[12,224,128]{2,1,0:T(8,128)(2,1)S(1)}, u32[]{:S(2)}) copy-start(bf16[12,224,128]{2,1,0:T(8,128)(2,1)S(1)} %collective-permute-done.2.halo_v) | copy-start | bytes 2064388
  114.3 4.9 %copy-start.19 = (f32[28]{0:T(128)S(1)}, f32[28]{0:T(128)}, u32[]{:S(2)}) copy-start(f32[28]{0:T(128)} %param.18) | copy-start | bytes 340
  114.3 5.1 %copy-start.15 = (bf16[512,128]{1,0:T(8,128)(2,1)S(1)}, bf16[512,128]{1,0:T(8,128)(2,1)}, u32[]{:S(2)}) copy-start(bf16[512,128]{1,0:T(8,128)(2,1)} %param.16) | copy-start | bytes 393220
  114.3 5.2 %copy-start.8 = (f32[512,28]{1,0:T(8,128)S(1)}, f32[512,28]{1,0:T(8,128)}, u32[]{:S(2)}) copy-start(f32[512,28]{1,0:T(8,128)} %copy-done.7) | copy-start | bytes 172036
  114.3 5.2 %copy-start.12 = (bf16[512,1792]{1,0:T(8,128)(2,1)S(1)}, bf16[512,1792]{1,0:T(8,128)(2,1)}, u32[]{:S(2)}) copy-start(bf16[512,1792]{1,0:T(8,128)(2,1)} %x_ref.3) | copy-start | bytes 5505028
  114.3 30.5 %all-to-all-start.3 = ((bf16[32,224,128]{2,1,0:T(8,128)(2,1)}), bf16[32,224,128]{2,1,0:T(8,128)(2,1)}, u32[]{:S(2)}, u32[]{:S(2)}) async-start(bf16[32,224,128]{2,1,0:T(8,128)(2,1)} %shard_map.119), calls=%async_computation.3 | async-start | bytes 3670016 | tf_op jit(solution)/shard_map/all_to_all | solution.py:413
  119.5 1.0 copy-start.10

commit v3 on v1

--- a/solution.py
+++ b/solution.py
@@ -14,6 +14,7 @@
 MOST_DOC = 1536
 BLOCK = 128
 TILE = 256
+GROUP = 2
 PLANE = ("x", "c", "y")
 CTX = ("z", "x", "c")
 
@@ -104,7 +105,7 @@
         in_specs=[pl.BlockSpec((step, ATT_HD, BLOCK), lambda i: (i, 0, 0))],
         out_specs=pl.BlockSpec((BLOCK, step * ATT_HD), lambda i: (0, i)),
         out_shape=jax.ShapeDtypeStruct((BLOCK, heads * ATT_HD), BF16),
-        compiler_params=compiler_params(),
+        compiler_params=compiler_params(16),
         cost_estimate=pl.CostEstimate(flops=0, bytes_accessed=4 * BLOCK * heads * ATT_HD, transcendentals=0),
     )(blocks)
 
@@ -135,8 +136,8 @@
     halo = halo_v.shape[0]
     own = q_ref.shape[0]
     per = TILE // BLOCK
-    pairs = own // per // 2
-    span = 2 * per
+    pairs = own // per // GROUP
+    span = GROUP * per
 
     def arriving(p):
         blocks = pl.ds(span * p, span)
@@ -171,7 +172,7 @@
     causal = down <= lax.broadcasted_iota(jnp.int32, (TILE, TILE), 1)
 
     def out_copy(p):
-        blocks = pl.ds(2 * per * p, 2 * per)
+        blocks = pl.ds(span * p, span)
         return pltpu.make_async_copy(o_own.at[blocks], o_ref.at[blocks], out_sems.at[p])
 
     def pair(p, _):
@@ -180,35 +181,48 @@
             copy.wait()
 
         def attend_over(reach):
-            first = 2 * p + halo // per + 1 - reach
+            first = GROUP * p + halo // per + 1 - reach
             rows = pl.multiple_of(first * TILE, TILE)
-            for half in range(2):
-                j = 2 * p + half
-                count = reach + half
-                q_t = jnp.concatenate([q_own[per * j + i] for i in range(per)], axis=1)
-                start = starts_ref[j]
-                scores = []
-                for i in range(count):
-                    s = dot(k_rows[pl.ds(rows + i * TILE, TILE), :], q_t)
-                    kept = down >= start - (j - count + 1 + i) * TILE
-                    if i == count - 1:
-                        kept = jnp.logical_and(kept, causal)
-                    scores.append(jnp.where(kept, s, -1e30))
-                top = scores[0]
-                for s in scores[1:]:
-                    top = jnp.maximum(top, s)
-                top = jnp.max(top, axis=0, keepdims=True)
-                total = jnp.zeros((TILE, TILE), F32)
+            starts = [starts_ref[GROUP * p + part] for part in range(GROUP)]
+            counts = [reach + part for part in range(GROUP)]
+
+            def score(part, i):
+                s = dot(k_rows[pl.ds(rows + i * TILE, TILE), :], queries)
+                kept = down >= starts[part] - (GROUP * p + part - counts[part] + 1 + i) * TILE
+                if i == counts[part] - 1:
+                    kept = jnp.logical_and(kept, causal)
+                return jnp.where(kept, s, -1e30)
+
+            def peak(scores):
+                tops = [jnp.max(jnp.reshape(s, (TILE // 8, 8, TILE)), axis=0) for s in scores]
+                return jnp.max(functools.reduce(jnp.maximum, tops), axis=0, keepdims=True)
+
+            def values(i):
+                return jnp.concatenate([v_cols[first * per + i * per + b] for b in range(per)], axis=1)
+
+            before, top = [], None
+            for part in range(GROUP + 1):
+                scores, waiting = [], None
+                total = jnp.zeros((8, TILE), F32)
                 mixed = jnp.zeros((ATT_HD, TILE), F32)
-                for i in range(count):
-                    weights = jnp.exp2((scores[i] - top) * factor)
-                    total = total + weights
-                    v_t = jnp.concatenate([v_cols[first * per + i * per + b] for b in range(per)], axis=1)
-                    mixed = mixed + dot(v_t, weights.astype(BF16))
-                total = jnp.sum(total, axis=0, keepdims=True)
-                out = (mixed * (1.0 / total)).astype(BF16)
-                for b in range(per):
-                    o_own[per * j + b] = out[:, b * BLOCK : (b + 1) * BLOCK]
+                if part < GROUP:
+                    queries = jnp.concatenate([q_own[per * (GROUP * p + part) + b] for b in range(per)], axis=1)
+                for i in range(counts[min(part, GROUP - 1)]):
+                    if part < GROUP:
+                        scores.append(score(part, i))
+                    if i < len(before):
+                        weights = jnp.exp2((before[i] - top) * factor)
+                        total = total + jnp.sum(jnp.reshape(weights, (TILE // 8, 8, TILE)), axis=0)
+                        if waiting is not None:
+                            mixed = mixed + dot(values(i - 1), waiting)
+                        waiting = weights.astype(BF16)
+                if part > 0:
+                    mixed = mixed + dot(values(len(before) - 1), waiting)
+                    out = (mixed * (1.0 / jnp.sum(total, axis=0, keepdims=True))).astype(BF16)
+                    for b in range(per):
+                        o_own[per * (GROUP * p + part - 1) + b] = out[:, b * BLOCK : (b + 1) * BLOCK]
+                if part < GROUP:
+                    before, top = scores, peak(scores)
 
         for count in range(1, most + 1):
             pl.when(reach == count)(functools.partial(attend_over, count))
@@ -231,7 +245,7 @@
     tiles = own // per
     most = halo // per + 1
     by_tile = jnp.reshape(starts, (tiles, 1, TILE))
-    reach = jnp.arange(0, tiles, 2, dtype=jnp.int32) - by_tile[::2, 0, 0] // TILE + 1
+    reach = jnp.arange(0, tiles, GROUP, dtype=jnp.int32) - by_tile[::GROUP, 0, 0] // TILE + 1
     vmem = pl.BlockSpec(memory_space=pltpu.VMEM)
     anywhere = pl.BlockSpec(memory_space=pl.ANY)
     return pl.pallas_call(
@@ -245,11 +259,11 @@
             pltpu.VMEM((own, ATT_HD, BLOCK), BF16),
             pltpu.VMEM((own, ATT_HD, BLOCK), BF16),
             pltpu.SemaphoreType.DMA((2,)),
-            pltpu.SemaphoreType.DMA((3, tiles // 2)),
-            pltpu.SemaphoreType.DMA((tiles // 2,)),
+            pltpu.SemaphoreType.DMA((3, tiles // GROUP)),
+            pltpu.SemaphoreType.DMA((tiles // GROUP,)),
         ],
         compiler_params=compiler_params(60),
-        cost_estimate=pl.CostEstimate(flops=4_000_000_000, bytes_accessed=8_000_000, transcendentals=4_000_000),
+        cost_estimate=pl.CostEstimate(flops=1_000_000, bytes_accessed=1_000_000, transcendentals=0),
     )(reach, by_tile, q_blocks, own_rows, own_v, halo_rows, halo_v)
 
 
@@ -266,7 +280,7 @@
     return dot(jnp.concatenate(split3(value), axis=1), wide_ref[...])
 
 
-def state_kernel(first_ref, start_ref, x_ref, step_ref, b_ref, rate_ref, wide_ref, out_ref, weight, passed):
+def state_kernel(first_ref, start_ref, x_ref, step_ref, b_ref, rate_ref, wide_ref, upper_ref, lower_ref, weight, passed):
     length = x_ref.shape[0]
     cumul = None
 
@@ -288,14 +302,15 @@
     fresh = lax.dot_general(b_same, high, over, preferred_element_type=F32) + lax.dot_general(
         b_same, low, over, preferred_element_type=F32
     )
-    states = fresh.shape[0]
-    out_ref[:states, :] = fresh
-    out_ref[states:, :] = spread(passed[...], wide_ref)
+    half = lower_ref.shape[0]
+    upper_ref[:half, :] = fresh[:half]
+    upper_ref[half:, :] = spread(passed[...], wide_ref)
+    lower_ref[...] = fresh[half:]
 
 
 def scan_kernel(
     first_ref, start_ref, x_ref, step_ref, b_ref, c_ref, rate_ref, wide_ref, skip_ref,
-    near_ref, far_ref, out_ref, weight, growth, g_high, g_low, c_open,
+    upper_ref, lower_ref, far_ref, out_ref, weight, growth, g_high, g_low, c_open,
 ):
     length = x_ref.shape[0]
     states = b_ref.shape[1]
@@ -317,7 +332,9 @@
 
     x = x_ref[...].astype(F32)
     high, low = split2(spread(weight[...], wide_ref) * x)
-    entering = near_ref[:states, :] + near_ref[states : states + 1, :] * far_ref[...]
+    half = lower_ref.shape[0]
+    near = jnp.concatenate([upper_ref[:half, :], lower_ref[...]], axis=0)
+    entering = near + upper_ref[half : half + 1, :] * far_ref[...]
     e_high, e_low = split2(entering)
     c = c_open[...]
     inner = dot(g_high[...], high) + dot(g_high[...], low) + dot(g_low[...], high) + dot(c, e_high) + dot(c, e_low)
@@ -340,29 +357,32 @@
     first = jnp.reshape(first, (1,)).astype(jnp.int32)
     smem = pl.BlockSpec(memory_space=pltpu.SMEM)
     columns = lambda rows: pl.BlockSpec((rows, chunk), lambda i: (0, i))
-    extra = 8
-    state = pl.pallas_call(
+    extra, half = 8, states // 2
+    upper, lower = pl.pallas_call(
         state_kernel,
         grid=(width // chunk,),
         in_specs=[
             smem, whole((length, 1)), columns(length), whole((length, heads)), whole((length, states)),
             whole((1, heads)), columns(3 * heads),
         ],
-        out_specs=columns(states + extra),
-        out_shape=jax.ShapeDtypeStruct((states + extra, width), F32),
+        out_specs=(columns(half + extra), columns(half)),
+        out_shape=(
+            jax.ShapeDtypeStruct((half + extra, width), F32),
+            jax.ShapeDtypeStruct((half, width), F32),
+        ),
         scratch_shapes=[pltpu.VMEM((length, heads), F32), pltpu.VMEM((extra, heads), F32)],
         compiler_params=compiler_params(16),
         cost_estimate=pl.CostEstimate(flops=2_000_000_000, bytes_accessed=3_000_000, transcendentals=20_000),
     )(first, start, x, step, b_group, rate, wide)
 
-    def finish(near, far):
+    def finish(near_upper, near_lower, far):
         return pl.pallas_call(
             scan_kernel,
             grid=(width // chunk,),
             in_specs=[
                 smem, whole((length, 1)), columns(length), whole((length, heads)), whole((length, states)),
                 whole((length, states)), whole((1, heads)), columns(3 * heads), columns(1),
-                columns(states + extra), columns(states),
+                columns(half + extra), columns(half), columns(states),
             ],
             out_specs=columns(length),
             out_shape=jax.ShapeDtypeStruct((length, width), BF16),
@@ -375,9 +395,10 @@
             ],
             compiler_params=compiler_params(16),
             cost_estimate=pl.CostEstimate(flops=5_000_000_000, bytes_accessed=6_000_000, transcendentals=40_000),
-        )(first, start, x, step, b_group, c_group, rate, wide, jnp.repeat(skip, width // heads)[None, :], near, far)
-
-    return state, finish
+        )(first, start, x, step, b_group, c_group, rate, wide, jnp.repeat(skip, width // heads)[None, :],
+            near_upper, near_lower, far)
+
+    return upper, lower, finish
 
 
 def doc_start(positions, doc_lengths):
@@ -409,26 +430,32 @@
     group = lax.axis_index("y") // (lax.axis_size("y") // M_GROUPS)
     b_group = lax.dynamic_slice_in_dim(in_proj_b, group * width, width, 1)
     c_group = lax.dynamic_slice_in_dim(out_proj_c, group * width, width, 1)
-    state, finish = scan_parts(ssm_input, step_size, b_group, c_group, decay_rate, skip_gain, start, first)
+    upper, lower, finish = scan_parts(ssm_input, step_size, b_group, c_group, decay_rate, skip_gain, start, first)
     starts = doc_start(plane_first + jnp.arange(plane_tokens), doc_lengths) - plane_first
-    v_blocks, state, starts = together((turn([values_in], 16), state, starts))
+    values_in, upper, lower = together((values_in, upper, lower))
+    to_next_block = [(i, i + 1) for i in range(devices - 1)]
+    near_upper = lax.ppermute(upper, CTX, to_next_block)
+    v_blocks, near_upper, starts = together((turn([values_in], 16), near_upper, starts))
 
     v = exchange(v_blocks)
-    near = lax.ppermute(state, CTX, [(i, i + 1) for i in range(devices - 1)])
-    two = state[:width] + state[width : width + 1] * near[:width]
     halo_k = lax.ppermute(k[-halo_blocks:], "z", to_next)
     own_rows = key_rows(k)
     halo_rows = key_rows(halo_k)
-    q_blocks, own_rows, halo_rows = together((turn([queries], 16), own_rows, halo_rows))
+    near_lower = lax.ppermute(lower, CTX, to_next_block)
+    q_blocks, own_rows, halo_rows, near_lower = together((turn([queries], 16), own_rows, halo_rows, near_lower))
 
     q = exchange(q_blocks)
     halo_v = lax.ppermute(v[-halo_blocks:], "z", to_next)
-    q, halo_v, two = together((q, halo_v, two))
+    half = lower.shape[0]
+    two = jnp.concatenate([upper[:half], lower], axis=0) + upper[half : half + 1] * jnp.concatenate(
+        [near_upper[:half], near_lower], axis=0
+    )
+    q, halo_v = together((q, halo_v))
 
     far = lax.ppermute(two, CTX, [(i, i + 2) for i in range(devices - 2)])
     o_blocks, far = together((attend(q, own_rows, v, halo_rows, halo_v, starts), far))
 
-    return turn_back(exchange(o_blocks)), finish(near, far)
+    return turn_back(exchange(o_blocks)), finish(near_upper, near_lower, far)
 
 
 def solution(mesh):

time: 157 us -> 147 us (0.936); the launches traced: 157 us -> 144 us
  waiting for transfers between devices: 61 us -> 52 us
  Pallas kernels: 40.8 us -> 37.1 us
  local copies, waits for them, and re-layouts: 15.3 us -> 12.5 us
  starting transfers between devices: 36.8 us -> 38.7 us
    all_to_all x4, waiting for transfers between devices: 30.5 us -> 18.2 us  [exchange(): lax.all_to_all(blocks, PLANE, split_axis=0, concat_axis=0, tiled=True)]
    ppermute x1, waiting for transfers between devices: 0.01 us -> 10.1 us  [local(): halo_v = lax.ppermute(v[-halo_blocks:], 'z', to_next)]
    ppermute x1 -> x2, waiting for transfers between devices: 21.9 us -> 16.8 us  [the longest x1 11 us: local(): near_upper = lax.ppermute(upper, CTX, to_next_block)]
    pallas_call x1, Pallas kernels: 15.4 us -> 10.9 us  [attend(): pl.pallas_call(functools.partial(attend_kernel, most), in_specs=[pl.Block...]
    unnamed x45 -> x35, local copies, waits for them, and re-layouts: 12.1 us -> 8.45 us
    ppermute x1 -> x2, starting transfers between devices: 2.03 us -> 4.1 us  [the longest x1 2.18 us: local(): near_upper = lax.ppermute(upper, CTX, to_next_block)]
    all_to_all x4, starting transfers between devices: 25.6 us -> 23.7 us  [exchange(): lax.all_to_all(blocks, PLANE, split_axis=0, concat_axis=0, tiled=True)]
    ppermute x1, waiting for transfers between devices: 8.66 us -> 6.83 us  [local(): halo_k = lax.ppermute(k[-halo_blocks:], 'z', to_next)]
  transfers between devices with their start and end apart: 8 -> 9, of which waited for: 5 -> 6; matrix products, arithmetic and copies ran while one was open for 3% -> 5% of each run, Pallas kernels for 23% -> 22%
where the time goes in v3:
time: 147 us; the launch traced here: 144 us
  waiting for transfers between devices  52 us (35%)
  starting transfers between devices  38.7 us (26%)
  Pallas kernels  37.1 us (25%)
  local copies, waits for them, and re-layouts  12.5 us (9%)
  other arithmetic  2.68 us (2%)
    all_to_all x4, starting transfers between devices, exchange(): lax.all_to_all(blocks, PLANE, split_axis=0, concat_axis=0, tiled=True)  23.7 us
    all_to_all x4, waiting for transfers between devices, exchange(): lax.all_to_all(blocks, PLANE, split_axis=0, concat_axis=0, tiled=True)  18.2 us
    ppermute x1, waiting for transfers between devices, local(): near_upper = lax.ppermute(upper, CTX, to_next_block)  11 us
    pallas_call x1, Pallas kernels, attend(): pl.pallas_call(functools.partial(attend_kernel, most), in_specs=[pl.Block...  10.9 us
    pallas_call x1, Pallas kernels, finish(): pl.pallas_call(scan_kernel, grid=(width // chunk,), in_specs=[smem, whole...  10.7 us
    ppermute x1, waiting for transfers between devices, local(): halo_v = lax.ppermute(v[-halo_blocks:], 'z', to_next)  10.1 us
    unnamed x35, local copies, waits for them, and re-layouts  8.45 us
    ppermute x1, waiting for transfers between devices, local(): halo_k = lax.ppermute(k[-halo_blocks:], 'z', to_next)  6.83 us
  transfers between devices with their start and end apart: 9, of which 6 were waited for; matrix products, arithmetic and copies ran while one was open for 5% of the time, Pallas kernels for 22%

profile of v3, /device:TPU:64, one launch (start us, length us, event | category | flops | bytes accessed | tf_op | source)
XLA Modules:
  0.0 144.1 jit_solution(3165874997707914130)
XLA Ops:
  0.6 2.6 %shard_map.116 = bf16[32,224,128]{2,1,0:T(8,128)(2,1)} custom-call(bf16[128,7168]{1,0:T(8,128)(2,1)} %refs_0_.4), custom_call_target="tpu_custom_call" | custom-call | bytes 3670016 | tf_op jit(solution)/shard_map/pallas_call | solution.py:78
  3.3 7.5 %all-to-all-start = ((bf16[32,224,128]{2,1,0:T(8,128)(2,1)}), bf16[32,224,128]{2,1,0:T(8,128)(2,1)S(1)}, u32[]{:S(2)}, u32[]{:S(2)}) async-start(bf16[32,224,128]{2,1,0:T(8,128)(2,1)} %shard_map.116), calls=%async_computation | async-start | bytes 3670016 | tf_op jit(solution)/shard_map/all_to_all | solution.py:410
  12.1 1.5 %copy-done.9 = bf16[512,1792]{1,0:T(8,128)(2,1)S(1)} copy-done((bf16[512,1792]{1,0:T(8,128)(2,1)S(1)}, bf16[512,1792]{1,0:T(8,128)(2,1)}, u32[]{:S(2)}) %copy-start.9) | copy-done | bytes 1835032
  13.6 4.8 %shard_map.113 = (f32[40,1792]{1,0:T(8,128)S(1)}, f32[32,1792]{1,0:T(8,128)S(1)}) custom-call(s32[1]{0:T(128)} %bitcast.first_ref, s32[512,1]{1,0:T(8,128)S(1)} %copy.21.start_ref, bf16[512,1792]{1,0:T(8,128)(2,1)S(1)} %copy-done.9, f32[512,28]{1,0:T(8,128)S(1)} %copy.22.step_ref, bf16[512,64]{1,0:T(8,128)(2,1)S(1)} %constant_dynamic-slice_fusion.1.b_ref, ...), custom_call_target="tpu_custom_call" | custom-call | flops 2000000000 | bytes 3000000 | tf_op jit(solution)/shard_map/pallas_call | solution.py:361
  18.4 2.2 %collective-permute-start = (f32[40,1792]{1,0:T(8,128)S(1)}, f32[40,1792]{1,0:T(8,128)}, u32[]{:S(2)}, u32[]{:S(2)}) collective-permute-start(f32[40,1792]{1,0:T(8,128)S(1)} %get-tuple-element.21), channel_id=1, source_target_pairs={{0,4},{4,8},{8,12},{12,16},{16,20},{20,24},{24,28},{28,32},{32,36}... | collective-permute-start | bytes 860168 | tf_op jit(solution)/shard_map/ppermute | solution.py:437
  20.9 1.5 %copy-done.5 = bf16[128,7168]{1,0:T(8,128)(2,1)S(1)} copy-done((bf16[128,7168]{1,0:T(8,128)(2,1)S(1)}, bf16[128,7168]{1,0:T(8,128)(2,1)}, u32[]{:S(2)}) %copy-start.5) | copy-done | bytes 1835032
  22.4 2.0 %shard_map.114 = bf16[32,224,128]{2,1,0:T(8,128)(2,1)S(1)} custom-call(bf16[128,7168]{1,0:T(8,128)(2,1)S(1)} %copy-done.5), custom_call_target="tpu_custom_call" | custom-call | bytes 3670016 | tf_op jit(solution)/shard_map/pallas_call | solution.py:78
  24.4 1.2 copy-done.3
  26.3 11.0 %collective-permute-done.upper_ref = f32[40,1792]{1,0:T(8,128)} collective-permute-done((f32[40,1792]{1,0:T(8,128)S(1)}, f32[40,1792]{1,0:T(8,128)}, u32[]{:S(2)}, u32[]{:S(2)}) %collective-permute-start) | collective-permute-done | bytes 286752 | tf_op jit(solution)/shard_map/ppermute | solution.py:437
  37.3 5.7 %all-to-all-start.2 = ((bf16[32,224,128]{2,1,0:T(8,128)(2,1)}), bf16[32,224,128]{2,1,0:T(8,128)(2,1)}, u32[]{:S(2)}, u32[]{:S(2)}) async-start(bf16[32,224,128]{2,1,0:T(8,128)(2,1)} %copy-done.3), calls=%async_computation.2 | async-start | bytes 3670016 | tf_op jit(solution)/shard_map/all_to_all | solution.py:410
  43.0 3.5 %collective-permute-start.1 = (bf16[12,224,128]{2,1,0:T(8,128)(2,1)S(1)}, bf16[12,224,128]{2,1,0:T(8,128)(2,1)S(1)}, u32[]{:S(2)}, u32[]{:S(2)}) collective-permute-start(bf16[12,224,128]{2,1,0:T(8,128)(2,1)S(1)} %slice.24), channel_id=1, source_target_pairs={{0,32},{32,64},{64,96},{1,33},{33,65},{65,97},{2,34},{34,66},{66,9... | collective-permute-start | bytes 2064392 | tf_op jit(solution)/shard_map/ppermute | solution.py:441
  46.6 1.9 %collective-permute-start.2 = (f32[32,1792]{1,0:T(8,128)S(1)}, f32[32,1792]{1,0:T(8,128)S(1)}, u32[]{:S(2)}, u32[]{:S(2)}) collective-permute-start(f32[32,1792]{1,0:T(8,128)S(1)} %get-tuple-element.23), channel_id=1, source_target_pairs={{0,4},{4,8},{8,12},{12,16},{16,20},{20,24},{24,28},{28,32},{32,36}... | collective-permute-start | bytes 688136 | tf_op jit(solution)/shard_map/ppermute | solution.py:444
  48.5 1.5 %copy-done.6 = bf16[128,7168]{1,0:T(8,128)(2,1)S(1)} copy-done((bf16[128,7168]{1,0:T(8,128)(2,1)S(1)}, bf16[128,7168]{1,0:T(8,128)(2,1)}, u32[]{:S(2)}) %copy-start.6) | copy-done | bytes 1835032
  50.0 2.0 %shard_map.115 = bf16[32,224,128]{2,1,0:T(8,128)(2,1)S(1)} custom-call(bf16[128,7168]{1,0:T(8,128)(2,1)S(1)} %copy-done.6), custom_call_target="tpu_custom_call" | custom-call | bytes 3670016 | tf_op jit(solution)/shard_map/pallas_call | solution.py:78
  52.0 1.2 copy-done.2
  53.3 1.0 shard_map.117.own_k
  54.3 1.3 copy-done.1
  55.6 6.8 %collective-permute-done.1.k_ref = bf16[12,224,128]{2,1,0:T(8,128)(2,1)S(1)} collective-permute-done((bf16[12,224,128]{2,1,0:T(8,128)(2,1)S(1)}, bf16[12,224,128]{2,1,0:T(8,128)(2,1)S(1)}, u32[]{:S(2)}, u32[]{:S(2)}) %collective-permute-start.1) | collective-permute-done | bytes 688160 | tf_op jit(solution)/shard_map/ppermute | solution.py:441
  62.9 5.8 %collective-permute-done.2.lower_ref = f32[32,1792]{1,0:T(8,128)S(1)} collective-permute-done((f32[32,1792]{1,0:T(8,128)S(1)}, f32[32,1792]{1,0:T(8,128)S(1)}, u32[]{:S(2)}, u32[]{:S(2)}) %collective-permute-start.2) | collective-permute-done | bytes 229408 | tf_op jit(solution)/shard_map/ppermute | solution.py:444
  68.7 5.7 %all-to-all-start.1 = ((bf16[32,224,128]{2,1,0:T(8,128)(2,1)}), bf16[32,224,128]{2,1,0:T(8,128)(2,1)}, u32[]{:S(2)}, u32[]{:S(2)}) async-start(bf16[32,224,128]{2,1,0:T(8,128)(2,1)} %copy-done.2), calls=%async_computation.1 | async-start | bytes 3670016 | tf_op jit(solution)/shard_map/all_to_all | solution.py:410
  74.4 1.0 slice.23
  75.4 1.1 slice.25
  76.5 3.5 %collective-permute-start.3 = (bf16[12,224,128]{2,1,0:T(8,128)(2,1)S(1)}, bf16[12,224,128]{2,1,0:T(8,128)(2,1)S(1)}, u32[]{:S(2)}, u32[]{:S(2)}) collective-permute-start(bf16[12,224,128]{2,1,0:T(8,128)(2,1)S(1)} %slice.25), channel_id=1, source_target_pairs={{0,32},{32,64},{64,96},{1,33},{33,65},{65,97},{2,34},{34,66},{66,9... | collective-permute-start | bytes 2064392 | tf_op jit(solution)/shard_map/ppermute | solution.py:448
  81.0 3.8 %collective-permute-start.4 = (f32[64,1792]{1,0:T(8,128)}, f32[64,1792]{1,0:T(8,128)}, u32[]{:S(2)}, u32[]{:S(2)}) collective-permute-start(f32[64,1792]{1,0:T(8,128)} %maximum_add_fusion), channel_id=1, source_target_pairs={{0,8},{4,12},{8,16},{12,20},{16,24},{20,28},{24,32},{28,36},{32,40... | collective-permute-start | bytes 1376264 | tf_op jit(solution)/shard_map/ppermute | solution.py:455
  84.8 0.9 slice_reduce_fusion.1
  86.3 10.1 %collective-permute-done.3.halo_v = bf16[12,224,128]{2,1,0:T(8,128)(2,1)S(1)} collective-permute-done((bf16[12,224,128]{2,1,0:T(8,128)(2,1)S(1)}, bf16[12,224,128]{2,1,0:T(8,128)(2,1)S(1)}, u32[]{:S(2)}, u32[]{:S(2)}) %collective-permute-start.3) | collective-permute-done | bytes 688160 | tf_op jit(solution)/shard_map/ppermute | solution.py:448
  96.4 3.6 %all-to-all-done.1.q_ref = bf16[32,224,128]{2,1,0:T(8,128)(2,1)} async-done(((bf16[32,224,128]{2,1,0:T(8,128)(2,1)}), bf16[32,224,128]{2,1,0:T(8,128)(2,1)}, u32[]{:S(2)}, u32[]{:S(2)}) %all-to-all-start.1) | async-done | bytes 1835040 | tf_op jit(solution)/shard_map/all_to_all | solution.py:410
  100.0 10.9 %shard_map.119 = bf16[32,224,128]{2,1,0:T(8,128)(2,1)} custom-call(s32[8]{0:T(128)} %subtract_add_fusion.reach_ref, s32[16,1,256]{2,1,0:T(1,128)} %bitcast.8, bf16[32,224,128]{2,1,0:T(8,128)(2,1)} %all-to-all-done.1.q_ref, bf16[4096,224]{1,0:T(8,128)(2,1)} %copy-done.1, bf16[32,224,128]{2,1,0:T(8,128)(2,1)} %all-to-all-done.2.own_v, ...), custom_call_target="tpu_custom_call" | custom-call | flops 1000000 | bytes 1000000 | tf_op jit(solution)/shard_map/pallas_call | solution.py:251
  111.0 4.9 %all-to-all-start.3 = ((bf16[32,224,128]{2,1,0:T(8,128)(2,1)}), bf16[32,224,128]{2,1,0:T(8,128)(2,1)}, u32[]{:S(2)}, u32[]{:S(2)}) async-start(bf16[32,224,128]{2,1,0:T(8,128)(2,1)} %shard_map.119), calls=%async_computation.3 | async-start | bytes 3670016 | tf_op jit(solution)/shard_map/all_to_all | solution.py:410
  116.2 10.7 %shard_map.121 = bf16[512,1792]{1,0:T(8,128)(2,1)} custom-call(s32[1]{0:T(128)} %bitcast.first_ref, s32[512,1]{1,0:T(8,128)S(1)} %copy.21.start_ref, bf16[512,1792]{1,0:T(8,128)(2,1)S(1)} %copy-done.10, f32[512,28]{1,0:T(8,128)S(1)} %copy.22.step_ref, bf16[512,64]{1,0:T(8,128)(2,1)S(1)} %copy-done.8, bf16[512,64]{1,0:T(8,128)(2,1)S(1)} %constant_dynamic-slice_fusion.c_ref, ...), custom_call_target="tpu_custom_call" | custom-call | flops 5000000000 | bytes 6000000 | tf_op jit(solution)/shard_map/pallas_call | solution.py:379
  126.8 14.6 %all-to-all-done.3.a_ref = bf16[32,224,128]{2,1,0:T(8,128)(2,1)} async-done(((bf16[32,224,128]{2,1,0:T(8,128)(2,1)}), bf16[32,224,128]{2,1,0:T(8,128)(2,1)}, u32[]{:S(2)}, u32[]{:S(2)}) %all-to-all-start.3) | async-done | bytes 1835040 | tf_op jit(solution)/shard_map/all_to_all | solution.py:410
  141.4 2.7 %shard_map.120 = bf16[128,7168]{1,0:T(8,128)(2,1)} custom-call(bf16[32,224,128]{2,1,0:T(8,128)(2,1)} %all-to-all-done.3.a_ref), custom_call_target="tpu_custom_call" | custom-call | bytes 3670016 | tf_op jit(solution)/shard_map/pallas_call | solution.py:102
  (56 shorter events, 4.4 us)
Async XLA Ops:
  0.6 11.3 %copy-start = (bf16[512,128]{1,0:T(8,128)(2,1)S(1)}, bf16[512,128]{1,0:T(8,128)(2,1)}, u32[]{:S(2)}) copy-start(bf16[512,128]{1,0:T(8,128)(2,1)} %param.15) | copy-start | bytes 393220
  3.2 7.5 %copy-start.15 = (s32[64]{0:T(128)S(1)}, s32[64]{0:T(128)}, u32[]{:S(2)}) copy-start(s32[64]{0:T(128)} %param.19) | copy-start | bytes 772
  3.3 8.5 %copy-start.14 = (f32[512,28]{0,1:T(8,128)S(1)}, f32[512,28]{0,1:T(8,128)}, u32[]{:S(2)}) copy-start(f32[512,28]{0,1:T(8,128)} %param.14) | copy-start | bytes 172036
  3.3 34.0 %all-to-all-start = ((bf16[32,224,128]{2,1,0:T(8,128)(2,1)}), bf16[32,224,128]{2,1,0:T(8,128)(2,1)S(1)}, u32[]{:S(2)}, u32[]{:S(2)}) async-start(bf16[32,224,128]{2,1,0:T(8,128)(2,1)} %shard_map.116), calls=%async_computation | async-start | bytes 3670016 | tf_op jit(solution)/shard_map/all_to_all | solution.py:410
  10.7 1.4 copy-start.11
  12.1 6.4 %copy-start.7 = (bf16[512,64]{1,0:T(8,128)(2,1)}, bf16[512,64]{1,0:T(8,128)(2,1)S(1)}, u32[]{:S(2)}) copy-start(bf16[512,64]{1,0:T(8,128)(2,1)S(1)} %constant_dynamic-slice_fusion.1.b_ref) | copy-start | bytes 196612
  12.1 1.5 %copy-start.9 = (bf16[512,1792]{1,0:T(8,128)(2,1)S(1)}, bf16[512,1792]{1,0:T(8,128)(2,1)}, u32[]{:S(2)}) copy-start(bf16[512,1792]{1,0:T(8,128)(2,1)} %x_ref.3) | copy-start | bytes 5505028
  18.4 18.8 %collective-permute-start = (f32[40,1792]{1,0:T(8,128)S(1)}, f32[40,1792]{1,0:T(8,128)}, u32[]{:S(2)}, u32[]{:S(2)}) collective-permute-start(f32[40,1792]{1,0:T(8,128)S(1)} %get-tuple-element.21), channel_id=1, source_target_pairs={{0,4},{4,8},{8,12},{12,16},{16,20},{20,24},{24,28},{28,32},{32,36}... | collective-permute-start | bytes 860168 | tf_op jit(solution)/shard_map/ppermute | solution.py:437
  20.9 1.5 %copy-start.5 = (bf16[128,7168]{1,0:T(8,128)(2,1)S(1)}, bf16[128,7168]{1,0:T(8,128)(2,1)}, u32[]{:S(2)}) copy-start(bf16[128,7168]{1,0:T(8,128)(2,1)} %refs_0_.2) | copy-start | bytes 5505028
  24.4 1.2 copy-start.3
  37.3 31.4 %all-to-all-start.2 = ((bf16[32,224,128]{2,1,0:T(8,128)(2,1)}), bf16[32,224,128]{2,1,0:T(8,128)(2,1)}, u32[]{:S(2)}, u32[]{:S(2)}) async-start(bf16[32,224,128]{2,1,0:T(8,128)(2,1)} %copy-done.3), calls=%async_computation.2 | async-start | bytes 3670016 | tf_op jit(solution)/shard_map/all_to_all | solution.py:410
  43.0 19.4 %collective-permute-start.1 = (bf16[12,224,128]{2,1,0:T(8,128)(2,1)S(1)}, bf16[12,224,128]{2,1,0:T(8,128)(2,1)S(1)}, u32[]{:S(2)}, u32[]{:S(2)}) collective-permute-start(bf16[12,224,128]{2,1,0:T(8,128)(2,1)S(1)} %slice.24), channel_id=1, source_target_pairs={{0,32},{32,64},{64,96},{1,33},{33,65},{65,97},{2,34},{34,66},{66,9... | collective-permute-start | bytes 2064392 | tf_op jit(solution)/shard_map/ppermute | solution.py:441
  46.6 22.1 %collective-permute-start.2 = (f32[32,1792]{1,0:T(8,128)S(1)}, f32[32,1792]{1,0:T(8,128)S(1)}, u32[]{:S(2)}, u32[]{:S(2)}) collective-permute-start(f32[32,1792]{1,0:T(8,128)S(1)} %get-tuple-element.23), channel_id=1, source_target_pairs={{0,4},{4,8},{8,12},{12,16},{16,20},{20,24},{24,28},{28,32},{32,36}... | collective-permute-start | bytes 688136 | tf_op jit(solution)/shard_map/ppermute | solution.py:444
  48.5 1.5 %copy-start.6 = (bf16[128,7168]{1,0:T(8,128)(2,1)S(1)}, bf16[128,7168]{1,0:T(8,128)(2,1)}, u32[]{:S(2)}) copy-start(bf16[128,7168]{1,0:T(8,128)(2,1)} %refs_0_.3) | copy-start | bytes 5505028
  52.0 1.2 copy-start.2
  54.3 1.3 copy-start.1
  62.9 5.8 %copy-start.4 = (bf16[1536,224]{1,0:T(8,128)(2,1)}, bf16[1536,224]{1,0:T(8,128)(2,1)S(1)}, u32[]{:S(2)}) copy-start(bf16[1536,224]{1,0:T(8,128)(2,1)S(1)} %shard_map.118.halo_k) | copy-start | bytes 2064388
  68.7 31.3 %all-to-all-start.1 = ((bf16[32,224,128]{2,1,0:T(8,128)(2,1)}), bf16[32,224,128]{2,1,0:T(8,128)(2,1)}, u32[]{:S(2)}, u32[]{:S(2)}) async-start(bf16[32,224,128]{2,1,0:T(8,128)(2,1)} %copy-done.2), calls=%async_computation.1 | async-start | bytes 3670016 | tf_op jit(solution)/shard_map/all_to_all | solution.py:410
  76.5 19.8 %collective-permute-start.3 = (bf16[12,224,128]{2,1,0:T(8,128)(2,1)S(1)}, bf16[12,224,128]{2,1,0:T(8,128)(2,1)S(1)}, u32[]{:S(2)}, u32[]{:S(2)}) collective-permute-start(bf16[12,224,128]{2,1,0:T(8,128)(2,1)S(1)} %slice.25), channel_id=1, source_target_pairs={{0,32},{32,64},{64,96},{1,33},{33,65},{65,97},{2,34},{34,66},{66,9... | collective-permute-start | bytes 2064392 | tf_op jit(solution)/shard_map/ppermute | solution.py:448
  81.0 30.0 %collective-permute-start.4 = (f32[64,1792]{1,0:T(8,128)}, f32[64,1792]{1,0:T(8,128)}, u32[]{:S(2)}, u32[]{:S(2)}) collective-permute-start(f32[64,1792]{1,0:T(8,128)} %maximum_add_fusion), channel_id=1, source_target_pairs={{0,8},{4,12},{8,16},{12,20},{16,24},{20,28},{24,32},{28,36},{32,40... | collective-permute-start | bytes 1376264 | tf_op jit(solution)/shard_map/ppermute | solution.py:455
  96.4 3.6 %copy-start.12 = (bf16[12,224,128]{2,1,0:T(8,128)(2,1)}, bf16[12,224,128]{2,1,0:T(8,128)(2,1)S(1)}, u32[]{:S(2)}) copy-start(bf16[12,224,128]{2,1,0:T(8,128)(2,1)S(1)} %collective-permute-done.3.halo_v) | copy-start | bytes 2064388
  110.9 4.9 %copy-start.16 = (f32[28]{0:T(128)S(1)}, f32[28]{0:T(128)}, u32[]{:S(2)}) copy-start(f32[28]{0:T(128)} %param.18) | copy-start | bytes 340
  110.9 5.1 %copy-start.13 = (bf16[512,128]{1,0:T(8,128)(2,1)S(1)}, bf16[512,128]{1,0:T(8,128)(2,1)}, u32[]{:S(2)}) copy-start(bf16[512,128]{1,0:T(8,128)(2,1)} %param.16) | copy-start | bytes 393220
  110.9 5.2 %copy-start.8 = (bf16[512,64]{1,0:T(8,128)(2,1)S(1)}, bf16[512,64]{1,0:T(8,128)(2,1)}, u32[]{:S(2)}) copy-start(bf16[512,64]{1,0:T(8,128)(2,1)} %copy-done.7) | copy-start | bytes 196612
  110.9 5.2 %copy-start.10 = (bf16[512,1792]{1,0:T(8,128)(2,1)S(1)}, bf16[512,1792]{1,0:T(8,128)(2,1)}, u32[]{:S(2)}) copy-start(bf16[512,1792]{1,0:T(8,128)(2,1)} %x_ref.3) | copy-start | bytes 5505028
  111.0 30.5 %all-to-all-start.3 = ((bf16[32,224,128]{2,1,0:T(8,128)(2,1)}), bf16[32,224,128]{2,1,0:T(8,128)(2,1)}, u32[]{:S(2)}, u32[]{:S(2)}) async-start(bf16[32,224,128]{2,1,0:T(8,128)(2,1)} %shard_map.119), calls=%async_computation.3 | async-start | bytes 3670016 | tf_op jit(solution)/shard_map/all_to_all | solution.py:410

commit v4 on v3

--- a/solution.py
+++ b/solution.py
@@ -440,9 +440,10 @@
     v = exchange(v_blocks)
     halo_k = lax.ppermute(k[-halo_blocks:], "z", to_next)
     own_rows = key_rows(k)
+    near_lower = lax.ppermute(lower, CTX, to_next_block)
+    queries, near_lower = together((queries, near_lower))
+    q_blocks, own_rows, halo_k = together((turn([queries], 16), own_rows, halo_k))
     halo_rows = key_rows(halo_k)
-    near_lower = lax.ppermute(lower, CTX, to_next_block)
-    q_blocks, own_rows, halo_rows, near_lower = together((turn([queries], 16), own_rows, halo_rows, near_lower))
 
     q = exchange(q_blocks)
     halo_v = lax.ppermute(v[-halo_blocks:], "z", to_next)

time: 147 us -> 155 us (1.054); the launches traced: 144 us -> 154 us
  waiting for transfers between devices: 52 us -> 58.6 us
  Pallas kernels: 37.1 us -> 39.1 us
    ppermute x1, waiting for transfers between devices: 5.78 us -> 20.3 us  [local(): near_lower = lax.ppermute(lower, CTX, to_next_block)]
    ppermute x1, waiting for transfers between devices: 6.83 us -> 0.01 us  [local(): halo_k = lax.ppermute(k[-halo_blocks:], 'z', to_next)]
    unnamed x35 -> x47, local copies, waits for them, and re-layouts: 8.45 us -> 10.7 us
    pallas_call x1, Pallas kernels: 10.9 us -> 12.9 us  [attend(): pl.pallas_call(functools.partial(attend_kernel, most), in_specs=[pl.Block...]
    ppermute x1, waiting for transfers between devices: 10.1 us -> 8.2 us  [local(): halo_v = lax.ppermute(v[-halo_blocks:], 'z', to_next)]
  transfers between devices with their start and end apart: 9 -> 9, of which waited for: 6 -> 5; matrix products, arithmetic and copies ran while one was open for 5% -> 4% of each run, Pallas kernels for 22% -> 22%
where the time goes in v4:
time: 155 us; the launch traced here: 154 us
  waiting for transfers between devices  58.6 us (38%)
  Pallas kernels  39.1 us (25%)
  starting transfers between devices  38.8 us (25%)
  local copies, waits for them, and re-layouts  13.3 us (9%)
  other arithmetic  3.04 us (2%)
    all_to_all x4, starting transfers between devices, exchange(): lax.all_to_all(blocks, PLANE, split_axis=0, concat_axis=0, tiled=True)  23.9 us
    ppermute x1, waiting for transfers between devices, local(): near_lower = lax.ppermute(lower, CTX, to_next_block)  20.3 us
    all_to_all x4, waiting for transfers between devices, exchange(): lax.all_to_all(blocks, PLANE, split_axis=0, concat_axis=0, tiled=True)  19.3 us
    pallas_call x1, Pallas kernels, attend(): pl.pallas_call(functools.partial(attend_kernel, most), in_specs=[pl.Block...  12.9 us
    ppermute x1, waiting for transfers between devices, local(): near_upper = lax.ppermute(upper, CTX, to_next_block)  10.8 us
    unnamed x47, local copies, waits for them, and re-layouts  10.7 us
    pallas_call x1, Pallas kernels, finish(): pl.pallas_call(scan_kernel, grid=(width // chunk,), in_specs=[smem, whole...  10.7 us
    ppermute x1, waiting for transfers between devices, local(): halo_v = lax.ppermute(v[-halo_blocks:], 'z', to_next)  8.2 us
  transfers between devices with their start and end apart: 9, of which 5 were waited for; matrix products, arithmetic and copies ran while one was open for 4% of the time, Pallas kernels for 22%

profile of v4, /device:TPU:64, one launch (start us, length us, event | category | flops | bytes accessed | tf_op | source)
XLA Modules:
  0.0 154.1 jit_solution(13771826327556433639)
XLA Ops:
  0.6 2.6 %shard_map.116 = bf16[32,224,128]{2,1,0:T(8,128)(2,1)} custom-call(bf16[128,7168]{1,0:T(8,128)(2,1)} %refs_0_.3), custom_call_target="tpu_custom_call" | custom-call | bytes 3670016 | tf_op jit(solution)/shard_map/pallas_call | solution.py:78
  3.3 7.5 %all-to-all-start = ((bf16[32,224,128]{2,1,0:T(8,128)(2,1)}), bf16[32,224,128]{2,1,0:T(8,128)(2,1)S(1)}, u32[]{:S(2)}, u32[]{:S(2)}) async-start(bf16[32,224,128]{2,1,0:T(8,128)(2,1)} %shard_map.116), calls=%async_computation | async-start | bytes 3670016 | tf_op jit(solution)/shard_map/all_to_all | solution.py:410
  12.1 1.5 copy-done.15
  13.6 4.8 %shard_map.113 = (f32[40,1792]{1,0:T(8,128)S(1)}, f32[32,1792]{1,0:T(8,128)S(1)}) custom-call(s32[1]{0:T(128)} %bitcast.first_ref, s32[512,1]{1,0:T(8,128)S(1)} %copy.21.start_ref, bf16[512,1792]{1,0:T(8,128)(2,1)S(1)} %copy-done.15, f32[512,28]{1,0:T(8,128)S(1)} %copy.22.step_ref, bf16[512,64]{1,0:T(8,128)(2,1)S(1)} %constant_dynamic-slice_fusion.1.b_ref, ...), custom_call_target="tpu_custom_call" | custom-call | flops 2000000000 | bytes 3000000 | tf_op jit(solution)/shard_map/pallas_call | solution.py:361
  19.1 2.2 %collective-permute-start = (f32[40,1792]{1,0:T(8,128)S(1)}, f32[40,1792]{1,0:T(8,128)S(1)}, u32[]{:S(2)}, u32[]{:S(2)}) collective-permute-start(f32[40,1792]{1,0:T(8,128)S(1)} %get-tuple-element.22), channel_id=1, source_target_pairs={{0,4},{4,8},{8,12},{12,16},{16,20},{20,24},{24,28},{28,32},{32,36}... | collective-permute-start | bytes 860168 | tf_op jit(solution)/shard_map/ppermute | solution.py:437
  21.6 1.5 copy-done.5
  23.1 2.0 %shard_map.114 = bf16[32,224,128]{2,1,0:T(8,128)(2,1)S(1)} custom-call(bf16[128,7168]{1,0:T(8,128)(2,1)S(1)} %copy-done.5), custom_call_target="tpu_custom_call" | custom-call | bytes 3670016 | tf_op jit(solution)/shard_map/pallas_call | solution.py:78
  25.1 1.2 copy-done.3
  26.3 10.8 %collective-permute-done.upper_ref = f32[40,1792]{1,0:T(8,128)S(1)} collective-permute-done((f32[40,1792]{1,0:T(8,128)S(1)}, f32[40,1792]{1,0:T(8,128)S(1)}, u32[]{:S(2)}, u32[]{:S(2)}) %collective-permute-start) | collective-permute-done | bytes 286752 | tf_op jit(solution)/shard_map/ppermute | solution.py:437
  37.2 0.7 copy-done.11
  37.9 5.7 %all-to-all-start.2 = ((bf16[32,224,128]{2,1,0:T(8,128)(2,1)}), bf16[32,224,128]{2,1,0:T(8,128)(2,1)}, u32[]{:S(2)}, u32[]{:S(2)}) async-start(bf16[32,224,128]{2,1,0:T(8,128)(2,1)} %copy-done.3), calls=%async_computation.2 | async-start | bytes 3670016 | tf_op jit(solution)/shard_map/all_to_all | solution.py:410
  43.6 3.5 %collective-permute-start.2 = (bf16[12,224,128]{2,1,0:T(8,128)(2,1)S(1)}, bf16[12,224,128]{2,1,0:T(8,128)(2,1)S(1)}, u32[]{:S(2)}, u32[]{:S(2)}) collective-permute-start(bf16[12,224,128]{2,1,0:T(8,128)(2,1)S(1)} %slice.24), channel_id=1, source_target_pairs={{0,32},{32,64},{64,96},{1,33},{33,65},{65,97},{2,34},{34,66},{66,9... | collective-permute-start | bytes 2064392 | tf_op jit(solution)/shard_map/ppermute | solution.py:441
  47.2 1.9 %collective-permute-start.1 = (f32[32,1792]{1,0:T(8,128)}, f32[32,1792]{1,0:T(8,128)}, u32[]{:S(2)}, u32[]{:S(2)}) collective-permute-start(f32[32,1792]{1,0:T(8,128)} %copy-done.7), channel_id=1, source_target_pairs={{0,4},{4,8},{8,12},{12,16},{16,20},{20,24},{24,28},{28,32},{32,36}... | collective-permute-start | bytes 688136 | tf_op jit(solution)/shard_map/ppermute | solution.py:443
  49.1 20.3 %collective-permute-done.1.lower_ref = f32[32,1792]{1,0:T(8,128)} collective-permute-done((f32[32,1792]{1,0:T(8,128)}, f32[32,1792]{1,0:T(8,128)}, u32[]{:S(2)}, u32[]{:S(2)}) %collective-permute-start.1) | collective-permute-done | bytes 229408 | tf_op jit(solution)/shard_map/ppermute | solution.py:443
  69.4 1.5 copy-done.6
  70.9 2.0 %shard_map.115 = bf16[32,224,128]{2,1,0:T(8,128)(2,1)S(1)} custom-call(bf16[128,7168]{1,0:T(8,128)(2,1)S(1)} %copy-done.6), custom_call_target="tpu_custom_call" | custom-call | bytes 3670016 | tf_op jit(solution)/shard_map/pallas_call | solution.py:78
  72.9 1.2 copy-done.2
  74.2 1.0 shard_map.117.own_k
  75.2 1.3 copy-done.1
  76.6 5.8 %all-to-all-start.1 = ((bf16[32,224,128]{2,1,0:T(8,128)(2,1)}), bf16[32,224,128]{2,1,0:T(8,128)(2,1)}, u32[]{:S(2)}, u32[]{:S(2)}) async-start(bf16[32,224,128]{2,1,0:T(8,128)(2,1)} %copy-done.2), calls=%async_computation.1 | async-start | bytes 3670016 | tf_op jit(solution)/shard_map/all_to_all | solution.py:410
  82.5 1.2 slice.25
  83.7 3.5 %collective-permute-start.3 = (bf16[12,224,128]{2,1,0:T(8,128)(2,1)S(1)}, bf16[12,224,128]{2,1,0:T(8,128)(2,1)}, u32[]{:S(2)}, u32[]{:S(2)}) collective-permute-start(bf16[12,224,128]{2,1,0:T(8,128)(2,1)S(1)} %slice.25), channel_id=1, source_target_pairs={{0,32},{32,64},{64,96},{1,33},{33,65},{65,97},{2,34},{34,66},{66,9... | collective-permute-start | bytes 2064392 | tf_op jit(solution)/shard_map/ppermute | solution.py:449
  87.3 1.8 %maximum_add_fusion = f32[64,1792]{1,0:T(8,128)} fusion(f32[32,1792]{1,0:T(8,128)S(1)} %copy-done.8, f32[32,1792]{1,0:T(8,128)S(1)} %slice.21, f32[32,1792]{1,0:T(8,128)} %collective-permute-done.1.lower_ref, f32[32,1792]{1,0:T(8,128)S(1)} %slice-done, f32[1792]{0:T(1024)S(1)} %slice_reduce_fusion), kind=kLoop, calls=%fused_computation.1 | loop fusion | flops 458752 | bytes 1383424 | tf_op jit(solution)/shard_map/add | solution.py:451
  89.1 3.8 %collective-permute-start.4 = (f32[64,1792]{1,0:T(8,128)}, f32[64,1792]{1,0:T(8,128)}, u32[]{:S(2)}, u32[]{:S(2)}) collective-permute-start(f32[64,1792]{1,0:T(8,128)} %maximum_add_fusion), channel_id=1, source_target_pairs={{0,8},{4,12},{8,16},{12,20},{16,24},{20,28},{24,32},{28,36},{32,40... | collective-permute-start | bytes 1376264 | tf_op jit(solution)/shard_map/ppermute | solution.py:456
  94.2 0.9 copy-done.4
  95.1 8.2 %collective-permute-done.3.halo_v = bf16[12,224,128]{2,1,0:T(8,128)(2,1)} collective-permute-done((bf16[12,224,128]{2,1,0:T(8,128)(2,1)S(1)}, bf16[12,224,128]{2,1,0:T(8,128)(2,1)}, u32[]{:S(2)}, u32[]{:S(2)}) %collective-permute-start.3) | collective-permute-done | bytes 688160 | tf_op jit(solution)/shard_map/ppermute | solution.py:449
  103.3 4.7 %all-to-all-done.1.q_ref = bf16[32,224,128]{2,1,0:T(8,128)(2,1)} async-done(((bf16[32,224,128]{2,1,0:T(8,128)(2,1)}), bf16[32,224,128]{2,1,0:T(8,128)(2,1)}, u32[]{:S(2)}, u32[]{:S(2)}) %all-to-all-start.1) | async-done | bytes 1835040 | tf_op jit(solution)/shard_map/all_to_all | solution.py:410
  108.0 12.9 %shard_map.119 = bf16[32,224,128]{2,1,0:T(8,128)(2,1)} custom-call(s32[8]{0:T(128)} %subtract_add_fusion.reach_ref, s32[16,1,256]{2,1,0:T(1,128)} %bitcast.8, bf16[32,224,128]{2,1,0:T(8,128)(2,1)} %all-to-all-done.1.q_ref, bf16[4096,224]{1,0:T(8,128)(2,1)} %copy-done.1, bf16[32,224,128]{2,1,0:T(8,128)(2,1)} %all-to-all-done.2.own_v, ...), custom_call_target="tpu_custom_call" | custom-call | flops 1000000 | bytes 1000000 | tf_op jit(solution)/shard_map/pallas_call | solution.py:251
  120.9 4.9 %all-to-all-start.3 = ((bf16[32,224,128]{2,1,0:T(8,128)(2,1)}), bf16[32,224,128]{2,1,0:T(8,128)(2,1)}, u32[]{:S(2)}, u32[]{:S(2)}) async-start(bf16[32,224,128]{2,1,0:T(8,128)(2,1)} %shard_map.119), calls=%async_computation.3 | async-start | bytes 3670016 | tf_op jit(solution)/shard_map/all_to_all | solution.py:410
  126.1 10.7 %shard_map.121 = bf16[512,1792]{1,0:T(8,128)(2,1)} custom-call(s32[1]{0:T(128)} %bitcast.first_ref, s32[512,1]{1,0:T(8,128)S(1)} %copy.21.start_ref, bf16[512,1792]{1,0:T(8,128)(2,1)S(1)} %copy-done.16, f32[512,28]{1,0:T(8,128)S(1)} %copy.22.step_ref, bf16[512,64]{1,0:T(8,128)(2,1)S(1)} %copy-done.14, bf16[512,64]{1,0:T(8,128)(2,1)S(1)} %constant_dynamic-slice_fusion.c_ref, ...), custom_call_target="tpu_custom_call" | custom-call | flops 5000000000 | bytes 6000000 | tf_op jit(solution)/shard_map/pallas_call | solution.py:379
  136.8 14.6 %all-to-all-done.3.a_ref = bf16[32,224,128]{2,1,0:T(8,128)(2,1)} async-done(((bf16[32,224,128]{2,1,0:T(8,128)(2,1)}), bf16[32,224,128]{2,1,0:T(8,128)(2,1)}, u32[]{:S(2)}, u32[]{:S(2)}) %all-to-all-start.3) | async-done | bytes 1835040 | tf_op jit(solution)/shard_map/all_to_all | solution.py:410
  151.4 2.7 %shard_map.120 = bf16[128,7168]{1,0:T(8,128)(2,1)} custom-call(bf16[32,224,128]{2,1,0:T(8,128)(2,1)} %all-to-all-done.3.a_ref), custom_call_target="tpu_custom_call" | custom-call | bytes 3670016 | tf_op jit(solution)/shard_map/pallas_call | solution.py:102
  (69 shorter events, 3.8 us)
Async XLA Ops:
  0.6 11.3 %copy-start = (bf16[512,128]{1,0:T(8,128)(2,1)S(1)}, bf16[512,128]{1,0:T(8,128)(2,1)}, u32[]{:S(2)}) copy-start(bf16[512,128]{1,0:T(8,128)(2,1)} %param.15) | copy-start | bytes 393220
  3.2 7.5 %copy-start.21 = (s32[64]{0:T(128)S(1)}, s32[64]{0:T(128)}, u32[]{:S(2)}) copy-start(s32[64]{0:T(128)} %param.19) | copy-start | bytes 772
  3.3 8.5 %copy-start.20 = (f32[512,28]{0,1:T(8,128)S(1)}, f32[512,28]{0,1:T(8,128)}, u32[]{:S(2)}) copy-start(f32[512,28]{0,1:T(8,128)} %param.14) | copy-start | bytes 172036
  3.3 33.9 %all-to-all-start = ((bf16[32,224,128]{2,1,0:T(8,128)(2,1)}), bf16[32,224,128]{2,1,0:T(8,128)(2,1)S(1)}, u32[]{:S(2)}, u32[]{:S(2)}) async-start(bf16[32,224,128]{2,1,0:T(8,128)(2,1)} %shard_map.116), calls=%async_computation | async-start | bytes 3670016 | tf_op jit(solution)/shard_map/all_to_all | solution.py:410
  10.7 1.4 copy-start.17
  12.1 6.4 %copy-start.13 = (bf16[512,64]{1,0:T(8,128)(2,1)}, bf16[512,64]{1,0:T(8,128)(2,1)S(1)}, u32[]{:S(2)}) copy-start(bf16[512,64]{1,0:T(8,128)(2,1)S(1)} %constant_dynamic-slice_fusion.1.b_ref) | copy-start | bytes 196612
  12.1 1.5 copy-start.15
  19.1 6.0 %copy-start.9 = (f32[40,1792]{1,0:T(8,128)}, f32[40,1792]{1,0:T(8,128)S(1)}, u32[]{:S(2)}) copy-start(f32[40,1792]{1,0:T(8,128)S(1)} %get-tuple-element.22) | copy-start | bytes 860164
  19.1 18.1 %collective-permute-start = (f32[40,1792]{1,0:T(8,128)S(1)}, f32[40,1792]{1,0:T(8,128)S(1)}, u32[]{:S(2)}, u32[]{:S(2)}) collective-permute-start(f32[40,1792]{1,0:T(8,128)S(1)} %get-tuple-element.22), channel_id=1, source_target_pairs={{0,4},{4,8},{8,12},{12,16},{16,20},{20,24},{24,28},{28,32},{32,36}... | collective-permute-start | bytes 860168 | tf_op jit(solution)/shard_map/ppermute | solution.py:437
  21.5 1.5 copy-start.5
  25.1 1.2 copy-start.3
  26.3 66.6 %copy-start.19 = (s32[4096]{0:T(1024)}, s32[4096]{0:T(1024)S(1)}, u32[]{:S(2)}) copy-start(s32[4096]{0:T(1024)S(1)} %broadcast_subtract_fusion) | copy-start | bytes 49156
  37.2 0.7 copy-start.11
  37.9 38.7 %all-to-all-start.2 = ((bf16[32,224,128]{2,1,0:T(8,128)(2,1)}), bf16[32,224,128]{2,1,0:T(8,128)(2,1)}, u32[]{:S(2)}, u32[]{:S(2)}) async-start(bf16[32,224,128]{2,1,0:T(8,128)(2,1)} %copy-done.3), calls=%async_computation.2 | async-start | bytes 3670016 | tf_op jit(solution)/shard_map/all_to_all | solution.py:410
  43.6 32.9 %collective-permute-start.2 = (bf16[12,224,128]{2,1,0:T(8,128)(2,1)S(1)}, bf16[12,224,128]{2,1,0:T(8,128)(2,1)S(1)}, u32[]{:S(2)}, u32[]{:S(2)}) collective-permute-start(bf16[12,224,128]{2,1,0:T(8,128)(2,1)S(1)} %slice.24), channel_id=1, source_target_pairs={{0,32},{32,64},{64,96},{1,33},{33,65},{65,97},{2,34},{34,66},{66,9... | collective-permute-start | bytes 2064392 | tf_op jit(solution)/shard_map/ppermute | solution.py:441
  47.2 22.2 %collective-permute-start.1 = (f32[32,1792]{1,0:T(8,128)}, f32[32,1792]{1,0:T(8,128)}, u32[]{:S(2)}, u32[]{:S(2)}) collective-permute-start(f32[32,1792]{1,0:T(8,128)} %copy-done.7), channel_id=1, source_target_pairs={{0,4},{4,8},{8,12},{12,16},{16,20},{20,24},{24,28},{28,32},{32,36}... | collective-permute-start | bytes 688136 | tf_op jit(solution)/shard_map/ppermute | solution.py:443
  69.4 1.5 copy-start.6
  72.9 1.2 copy-start.2
  75.2 1.3 copy-start.1
  76.5 5.9 %copy-start.10 = (f32[40,1792]{1,0:T(8,128)S(1)}, f32[40,1792]{1,0:T(8,128)}, u32[]{:S(2)}) copy-start(f32[40,1792]{1,0:T(8,128)} %copy-done.9) | copy-start | bytes 860164
  76.6 31.4 %all-to-all-start.1 = ((bf16[32,224,128]{2,1,0:T(8,128)(2,1)}), bf16[32,224,128]{2,1,0:T(8,128)(2,1)}, u32[]{:S(2)}, u32[]{:S(2)}) async-start(bf16[32,224,128]{2,1,0:T(8,128)(2,1)} %copy-done.2), calls=%async_computation.1 | async-start | bytes 3670016 | tf_op jit(solution)/shard_map/all_to_all | solution.py:410
  82.4 4.9 %copy-start.8 = (f32[32,1792]{1,0:T(8,128)S(1)}, f32[32,1792]{1,0:T(8,128)}, u32[]{:S(2)}) copy-start(f32[32,1792]{1,0:T(8,128)} %copy-done.7) | copy-start | bytes 688132
  82.4 4.9 %slice-start = ((f32[40,1792]{1,0:T(8,128)}), f32[32,1792]{1,0:T(8,128)S(1)}, s32[]{:S(2)}) async-start(f32[40,1792]{1,0:T(8,128)} %copy-done.11), calls=%async_computation.4 | async-start | bytes 458752 | tf_op jit(solution)/shard_map/slice | solution.py:452
  83.7 19.6 %collective-permute-start.3 = (bf16[12,224,128]{2,1,0:T(8,128)(2,1)S(1)}, bf16[12,224,128]{2,1,0:T(8,128)(2,1)}, u32[]{:S(2)}, u32[]{:S(2)}) collective-permute-start(bf16[12,224,128]{2,1,0:T(8,128)(2,1)S(1)} %slice.25), channel_id=1, source_target_pairs={{0,32},{32,64},{64,96},{1,33},{33,65},{65,97},{2,34},{34,66},{66,9... | collective-permute-start | bytes 2064392 | tf_op jit(solution)/shard_map/ppermute | solution.py:449
  89.1 31.8 %collective-permute-start.4 = (f32[64,1792]{1,0:T(8,128)}, f32[64,1792]{1,0:T(8,128)}, u32[]{:S(2)}, u32[]{:S(2)}) collective-permute-start(f32[64,1792]{1,0:T(8,128)} %maximum_add_fusion), channel_id=1, source_target_pairs={{0,8},{4,12},{8,16},{12,20},{16,24},{20,28},{24,32},{28,36},{32,40... | collective-permute-start | bytes 1376264 | tf_op jit(solution)/shard_map/ppermute | solution.py:456
  94.2 0.9 copy-start.4
  120.9 4.9 %copy-start.22 = (f32[28]{0:T(128)S(1)}, f32[28]{0:T(128)}, u32[]{:S(2)}) copy-start(f32[28]{0:T(128)} %param.18) | copy-start | bytes 340
  120.9 5.1 %copy-start.18 = (bf16[512,128]{1,0:T(8,128)(2,1)S(1)}, bf16[512,128]{1,0:T(8,128)(2,1)}, u32[]{:S(2)}) copy-start(bf16[512,128]{1,0:T(8,128)(2,1)} %param.16) | copy-start | bytes 393220
  120.9 5.2 %copy-start.12 = (f32[40,1792]{1,0:T(8,128)S(1)}, f32[40,1792]{1,0:T(8,128)}, u32[]{:S(2)}) copy-start(f32[40,1792]{1,0:T(8,128)} %copy-done.11) | copy-start | bytes 860164
  120.9 5.2 %copy-start.14 = (bf16[512,64]{1,0:T(8,128)(2,1)S(1)}, bf16[512,64]{1,0:T(8,128)(2,1)}, u32[]{:S(2)}) copy-start(bf16[512,64]{1,0:T(8,128)(2,1)} %copy-done.13) | copy-start | bytes 196612
  120.9 5.2 %copy-start.16 = (bf16[512,1792]{1,0:T(8,128)(2,1)S(1)}, bf16[512,1792]{1,0:T(8,128)(2,1)}, u32[]{:S(2)}) copy-start(bf16[512,1792]{1,0:T(8,128)(2,1)} %x_ref.3) | copy-start | bytes 5505028
  120.9 30.4 %all-to-all-start.3 = ((bf16[32,224,128]{2,1,0:T(8,128)(2,1)}), bf16[32,224,128]{2,1,0:T(8,128)(2,1)}, u32[]{:S(2)}, u32[]{:S(2)}) async-start(bf16[32,224,128]{2,1,0:T(8,128)(2,1)} %shard_map.119), calls=%async_computation.3 | async-start | bytes 3670016 | tf_op jit(solution)/shard_map/all_to_all | solution.py:410
  (1 other events, 0.7 us)

commit v5 on v3

--- a/solution.py
+++ b/solution.py
@@ -302,7 +302,7 @@
     fresh = lax.dot_general(b_same, high, over, preferred_element_type=F32) + lax.dot_general(
         b_same, low, over, preferred_element_type=F32
     )
-    half = lower_ref.shape[0]
+    half = fresh.shape[0] - lower_ref.shape[0]
     upper_ref[:half, :] = fresh[:half]
     upper_ref[half:, :] = spread(passed[...], wide_ref)
     lower_ref[...] = fresh[half:]
@@ -332,7 +332,7 @@
 
     x = x_ref[...].astype(F32)
     high, low = split2(spread(weight[...], wide_ref) * x)
-    half = lower_ref.shape[0]
+    half = states - lower_ref.shape[0]
     near = jnp.concatenate([upper_ref[:half, :], lower_ref[...]], axis=0)
     entering = near + upper_ref[half : half + 1, :] * far_ref[...]
     e_high, e_low = split2(entering)
@@ -357,7 +357,7 @@
     first = jnp.reshape(first, (1,)).astype(jnp.int32)
     smem = pl.BlockSpec(memory_space=pltpu.SMEM)
     columns = lambda rows: pl.BlockSpec((rows, chunk), lambda i: (0, i))
-    extra, half = 8, states // 2
+    extra, half = 8, states * 3 // 4
     upper, lower = pl.pallas_call(
         state_kernel,
         grid=(width // chunk,),
@@ -365,10 +365,10 @@
             smem, whole((length, 1)), columns(length), whole((length, heads)), whole((length, states)),
             whole((1, heads)), columns(3 * heads),
         ],
-        out_specs=(columns(half + extra), columns(half)),
+        out_specs=(columns(half + extra), columns(states - half)),
         out_shape=(
             jax.ShapeDtypeStruct((half + extra, width), F32),
-            jax.ShapeDtypeStruct((half, width), F32),
+            jax.ShapeDtypeStruct((states - half, width), F32),
         ),
         scratch_shapes=[pltpu.VMEM((length, heads), F32), pltpu.VMEM((extra, heads), F32)],
         compiler_params=compiler_params(16),
@@ -382,7 +382,7 @@
             in_specs=[
                 smem, whole((length, 1)), columns(length), whole((length, heads)), whole((length, states)),
                 whole((length, states)), whole((1, heads)), columns(3 * heads), columns(1),
-                columns(half + extra), columns(half), columns(states),
+                columns(half + extra), columns(states - half), columns(states),
             ],
             out_specs=columns(length),
             out_shape=jax.ShapeDtypeStruct((length, width), BF16),
@@ -446,7 +446,7 @@
 
     q = exchange(q_blocks)
     halo_v = lax.ppermute(v[-halo_blocks:], "z", to_next)
-    half = lower.shape[0]
+    half = width - lower.shape[0]
     two = jnp.concatenate([upper[:half], lower], axis=0) + upper[half : half + 1] * jnp.concatenate(
         [near_upper[:half], near_lower], axis=0
     )

time: 147 us -> 148 us (level); the launches traced: 144 us -> 147 us
  Pallas kernels: 37.1 us -> 40.1 us
    pallas_call x1, Pallas kernels: 10.9 us -> 14.1 us  [attend(): pl.pallas_call(functools.partial(attend_kernel, most), in_specs=[pl.Block...]
    unnamed x35 -> x39, local copies, waits for them, and re-layouts: 8.45 us -> 10.6 us
  transfers between devices with their start and end apart: 9 -> 9, of which waited for: 6 -> 7; matrix products, arithmetic and copies ran while one was open for 5% -> 3% of each run, Pallas kernels for 22% -> 24%
where the time goes in v5:
time: 148 us; the launch traced here: 147 us
  waiting for transfers between devices  53.1 us (36%)
  Pallas kernels  40.1 us (27%)
  starting transfers between devices  37.7 us (25%)
  local copies, waits for them, and re-layouts  13 us (9%)
  other arithmetic  2.14 us (1%)
    all_to_all x4, starting transfers between devices, exchange(): lax.all_to_all(blocks, PLANE, split_axis=0, concat_axis=0, tiled=True)  22.8 us
    all_to_all x4, waiting for transfers between devices, exchange(): lax.all_to_all(blocks, PLANE, split_axis=0, concat_axis=0, tiled=True)  19.1 us
    pallas_call x1, Pallas kernels, attend(): pl.pallas_call(functools.partial(attend_kernel, most), in_specs=[pl.Block...  14.1 us
    ppermute x1, waiting for transfers between devices, local(): near_upper = lax.ppermute(upper, CTX, to_next_block)  12.1 us
    unnamed x39, local copies, waits for them, and re-layouts  10.6 us
    pallas_call x1, Pallas kernels, finish(): pl.pallas_call(scan_kernel, grid=(width // chunk,), in_specs=[smem, whole...  10.6 us
    ppermute x1, waiting for transfers between devices, local(): halo_v = lax.ppermute(v[-halo_blocks:], 'z', to_next)  10.4 us
    ppermute x1, waiting for transfers between devices, local(): halo_k = lax.ppermute(k[-halo_blocks:], 'z', to_next)  6.82 us
  transfers between devices with their start and end apart: 9, of which 7 were waited for; matrix products, arithmetic and copies ran while one was open for 3% of the time, Pallas kernels for 24%

profile of v5, /device:TPU:64, one launch (start us, length us, event | category | flops | bytes accessed | tf_op | source)
XLA Modules:
  0.0 147.3 jit_solution(2139838112260707311)
XLA Ops:
  0.6 2.6 %shard_map.116 = bf16[32,224,128]{2,1,0:T(8,128)(2,1)} custom-call(bf16[128,7168]{1,0:T(8,128)(2,1)} %refs_0_.4), custom_call_target="tpu_custom_call" | custom-call | bytes 3670016 | tf_op jit(solution)/shard_map/pallas_call | solution.py:78
  3.3 7.5 %all-to-all-start = ((bf16[32,224,128]{2,1,0:T(8,128)(2,1)}), bf16[32,224,128]{2,1,0:T(8,128)(2,1)S(1)}, u32[]{:S(2)}, u32[]{:S(2)}) async-start(bf16[32,224,128]{2,1,0:T(8,128)(2,1)} %shard_map.116), calls=%async_computation | async-start | bytes 3670016 | tf_op jit(solution)/shard_map/all_to_all | solution.py:410
  12.1 1.5 %copy-done.11 = bf16[512,1792]{1,0:T(8,128)(2,1)S(1)} copy-done((bf16[512,1792]{1,0:T(8,128)(2,1)S(1)}, bf16[512,1792]{1,0:T(8,128)(2,1)}, u32[]{:S(2)}) %copy-start.11) | copy-done | bytes 1835032
  13.6 4.7 %shard_map.113 = (f32[56,1792]{1,0:T(8,128)S(1)}, f32[16,1792]{1,0:T(8,128)S(1)}) custom-call(s32[1]{0:T(128)} %bitcast.first_ref, s32[512,1]{1,0:T(8,128)S(1)} %copy.21.start_ref, bf16[512,1792]{1,0:T(8,128)(2,1)S(1)} %copy-done.11, f32[512,28]{1,0:T(8,128)S(1)} %copy.22.step_ref, bf16[512,64]{1,0:T(8,128)(2,1)S(1)} %constant_dynamic-slice_fusion.1.b_ref, ...), custom_call_target="tpu_custom_call" | custom-call | flops 2000000000 | bytes 3000000 | tf_op jit(solution)/shard_map/pallas_call | solution.py:361
  19.0 2.2 %collective-permute-start = (f32[56,1792]{1,0:T(8,128)S(1)}, f32[56,1792]{1,0:T(8,128)S(1)}, u32[]{:S(2)}, u32[]{:S(2)}) collective-permute-start(f32[56,1792]{1,0:T(8,128)S(1)} %get-tuple-element.21), channel_id=1, source_target_pairs={{0,4},{4,8},{8,12},{12,16},{16,20},{20,24},{24,28},{28,32},{32,36}... | collective-permute-start | bytes 1204232 | tf_op jit(solution)/shard_map/ppermute | solution.py:437
  21.2 1.5 %copy-done.5 = bf16[128,7168]{1,0:T(8,128)(2,1)S(1)} copy-done((bf16[128,7168]{1,0:T(8,128)(2,1)S(1)}, bf16[128,7168]{1,0:T(8,128)(2,1)}, u32[]{:S(2)}) %copy-start.5) | copy-done | bytes 1835032
  22.7 2.0 %shard_map.114 = bf16[32,224,128]{2,1,0:T(8,128)(2,1)S(1)} custom-call(bf16[128,7168]{1,0:T(8,128)(2,1)S(1)} %copy-done.5), custom_call_target="tpu_custom_call" | custom-call | bytes 3670016 | tf_op jit(solution)/shard_map/pallas_call | solution.py:78
  24.8 1.2 copy-done.3
  26.3 12.1 %collective-permute-done.upper_ref = f32[56,1792]{1,0:T(8,128)S(1)} collective-permute-done((f32[56,1792]{1,0:T(8,128)S(1)}, f32[56,1792]{1,0:T(8,128)S(1)}, u32[]{:S(2)}, u32[]{:S(2)}) %collective-permute-start) | collective-permute-done | bytes 401440 | tf_op jit(solution)/shard_map/ppermute | solution.py:437
  38.4 5.7 %all-to-all-start.2 = ((bf16[32,224,128]{2,1,0:T(8,128)(2,1)}), bf16[32,224,128]{2,1,0:T(8,128)(2,1)}, u32[]{:S(2)}, u32[]{:S(2)}) async-start(bf16[32,224,128]{2,1,0:T(8,128)(2,1)} %copy-done.3), calls=%async_computation.2 | async-start | bytes 3670016 | tf_op jit(solution)/shard_map/all_to_all | solution.py:410
  44.2 3.5 %collective-permute-start.1 = (bf16[12,224,128]{2,1,0:T(8,128)(2,1)S(1)}, bf16[12,224,128]{2,1,0:T(8,128)(2,1)S(1)}, u32[]{:S(2)}, u32[]{:S(2)}) collective-permute-start(bf16[12,224,128]{2,1,0:T(8,128)(2,1)S(1)} %slice.24), channel_id=1, source_target_pairs={{0,32},{32,64},{64,96},{1,33},{33,65},{65,97},{2,34},{34,66},{66,9... | collective-permute-start | bytes 2064392 | tf_op jit(solution)/shard_map/ppermute | solution.py:441
  47.7 1.9 %collective-permute-start.2 = (f32[16,1792]{1,0:T(8,128)}, f32[16,1792]{1,0:T(8,128)}, u32[]{:S(2)}, u32[]{:S(2)}) collective-permute-start(f32[16,1792]{1,0:T(8,128)} %copy-done.9), channel_id=1, source_target_pairs={{0,4},{4,8},{8,12},{12,16},{16,20},{20,24},{24,28},{28,32},{32,36}... | collective-permute-start | bytes 344072 | tf_op jit(solution)/shard_map/ppermute | solution.py:444
  49.6 1.5 %copy-done.6 = bf16[128,7168]{1,0:T(8,128)(2,1)S(1)} copy-done((bf16[128,7168]{1,0:T(8,128)(2,1)S(1)}, bf16[128,7168]{1,0:T(8,128)(2,1)}, u32[]{:S(2)}) %copy-start.6) | copy-done | bytes 1835032
  51.1 2.0 %shard_map.115 = bf16[32,224,128]{2,1,0:T(8,128)(2,1)S(1)} custom-call(bf16[128,7168]{1,0:T(8,128)(2,1)S(1)} %copy-done.6), custom_call_target="tpu_custom_call" | custom-call | bytes 3670016 | tf_op jit(solution)/shard_map/pallas_call | solution.py:78
  53.2 1.2 copy-done.2
  54.4 1.0 shard_map.117.own_k
  55.5 1.3 copy-done.1
  56.8 6.8 %collective-permute-done.1.k_ref = bf16[12,224,128]{2,1,0:T(8,128)(2,1)S(1)} collective-permute-done((bf16[12,224,128]{2,1,0:T(8,128)(2,1)S(1)}, bf16[12,224,128]{2,1,0:T(8,128)(2,1)S(1)}, u32[]{:S(2)}, u32[]{:S(2)}) %collective-permute-start.1) | collective-permute-done | bytes 688160 | tf_op jit(solution)/shard_map/ppermute | solution.py:441
  64.0 4.7 %collective-permute-done.2.lower_ref = f32[16,1792]{1,0:T(8,128)} collective-permute-done((f32[16,1792]{1,0:T(8,128)}, f32[16,1792]{1,0:T(8,128)}, u32[]{:S(2)}, u32[]{:S(2)}) %collective-permute-start.2) | collective-permute-done | bytes 114720 | tf_op jit(solution)/shard_map/ppermute | solution.py:444
  68.7 1.0 all-to-all-done.2.own_v
  69.7 4.7 %all-to-all-start.1 = ((bf16[32,224,128]{2,1,0:T(8,128)(2,1)}), bf16[32,224,128]{2,1,0:T(8,128)(2,1)}, u32[]{:S(2)}, u32[]{:S(2)}) async-start(bf16[32,224,128]{2,1,0:T(8,128)(2,1)} %copy-done.2), calls=%async_computation.1 | async-start | bytes 3670016 | tf_op jit(solution)/shard_map/all_to_all | solution.py:410
  74.6 1.1 slice.25
  75.7 3.5 %collective-permute-start.3 = (bf16[12,224,128]{2,1,0:T(8,128)(2,1)S(1)}, bf16[12,224,128]{2,1,0:T(8,128)(2,1)}, u32[]{:S(2)}, u32[]{:S(2)}) collective-permute-start(bf16[12,224,128]{2,1,0:T(8,128)(2,1)S(1)} %slice.25), channel_id=1, source_target_pairs={{0,32},{32,64},{64,96},{1,33},{33,65},{65,97},{2,34},{34,66},{66,9... | collective-permute-start | bytes 2064392 | tf_op jit(solution)/shard_map/ppermute | solution.py:448
  80.2 3.8 %collective-permute-start.4 = (f32[64,1792]{1,0:T(8,128)S(1)}, f32[64,1792]{1,0:T(8,128)S(1)}, u32[]{:S(2)}, u32[]{:S(2)}) collective-permute-start(f32[64,1792]{1,0:T(8,128)S(1)} %maximum_add_fusion), channel_id=1, source_target_pairs={{0,8},{4,12},{8,16},{12,20},{16,24},{20,28},{24,32},{28,36},{32,40... | collective-permute-start | bytes 1376264 | tf_op jit(solution)/shard_map/ppermute | solution.py:455
  84.8 10.4 %collective-permute-done.3.halo_v = bf16[12,224,128]{2,1,0:T(8,128)(2,1)} collective-permute-done((bf16[12,224,128]{2,1,0:T(8,128)(2,1)S(1)}, bf16[12,224,128]{2,1,0:T(8,128)(2,1)}, u32[]{:S(2)}, u32[]{:S(2)}) %collective-permute-start.3) | collective-permute-done | bytes 688160 | tf_op jit(solution)/shard_map/ppermute | solution.py:448
  95.2 4.8 %all-to-all-done.1.q_ref = bf16[32,224,128]{2,1,0:T(8,128)(2,1)} async-done(((bf16[32,224,128]{2,1,0:T(8,128)(2,1)}), bf16[32,224,128]{2,1,0:T(8,128)(2,1)}, u32[]{:S(2)}, u32[]{:S(2)}) %all-to-all-start.1) | async-done | bytes 1835040 | tf_op jit(solution)/shard_map/all_to_all | solution.py:410
  100.0 14.1 %shard_map.119 = bf16[32,224,128]{2,1,0:T(8,128)(2,1)} custom-call(s32[8]{0:T(128)} %subtract_add_fusion.reach_ref, s32[16,1,256]{2,1,0:T(1,128)} %bitcast.8, bf16[32,224,128]{2,1,0:T(8,128)(2,1)} %all-to-all-done.1.q_ref, bf16[4096,224]{1,0:T(8,128)(2,1)} %copy-done.1, bf16[32,224,128]{2,1,0:T(8,128)(2,1)} %all-to-all-done.2.own_v, ...), custom_call_target="tpu_custom_call" | custom-call | flops 1000000 | bytes 1000000 | tf_op jit(solution)/shard_map/pallas_call | solution.py:251
  114.1 4.9 %all-to-all-start.3 = ((bf16[32,224,128]{2,1,0:T(8,128)(2,1)}), bf16[32,224,128]{2,1,0:T(8,128)(2,1)}, u32[]{:S(2)}, u32[]{:S(2)}) async-start(bf16[32,224,128]{2,1,0:T(8,128)(2,1)} %shard_map.119), calls=%async_computation.3 | async-start | bytes 3670016 | tf_op jit(solution)/shard_map/all_to_all | solution.py:410
  119.3 1.5 %copy-done.12 = bf16[512,1792]{1,0:T(8,128)(2,1)S(1)} copy-done((bf16[512,1792]{1,0:T(8,128)(2,1)S(1)}, bf16[512,1792]{1,0:T(8,128)(2,1)}, u32[]{:S(2)}) %copy-start.12) | copy-done | bytes 1835032
  120.8 10.6 %shard_map.121 = bf16[512,1792]{1,0:T(8,128)(2,1)} custom-call(s32[1]{0:T(128)} %bitcast.first_ref, s32[512,1]{1,0:T(8,128)S(1)} %copy-done.8, bf16[512,1792]{1,0:T(8,128)(2,1)S(1)} %copy-done.12, f32[512,28]{1,0:T(8,128)S(1)} %copy.22.step_ref, bf16[512,64]{1,0:T(8,128)(2,1)S(1)} %constant_dynamic-slice_fusion.1.b_ref, ...), custom_call_target="tpu_custom_call" | custom-call | flops 5000000000 | bytes 6000000 | tf_op jit(solution)/shard_map/pallas_call | solution.py:379
  131.4 13.2 %all-to-all-done.3.a_ref = bf16[32,224,128]{2,1,0:T(8,128)(2,1)} async-done(((bf16[32,224,128]{2,1,0:T(8,128)(2,1)}), bf16[32,224,128]{2,1,0:T(8,128)(2,1)}, u32[]{:S(2)}, u32[]{:S(2)}) %all-to-all-start.3) | async-done | bytes 1835040 | tf_op jit(solution)/shard_map/all_to_all | solution.py:410
  144.6 2.7 %shard_map.120 = bf16[128,7168]{1,0:T(8,128)(2,1)} custom-call(bf16[32,224,128]{2,1,0:T(8,128)(2,1)} %all-to-all-done.3.a_ref), custom_call_target="tpu_custom_call" | custom-call | bytes 3670016 | tf_op jit(solution)/shard_map/pallas_call | solution.py:102
  (60 shorter events, 4.7 us)
Async XLA Ops:
  0.6 11.3 %copy-start = (bf16[512,128]{1,0:T(8,128)(2,1)S(1)}, bf16[512,128]{1,0:T(8,128)(2,1)}, u32[]{:S(2)}) copy-start(bf16[512,128]{1,0:T(8,128)(2,1)} %param.15) | copy-start | bytes 393220
  3.2 7.5 %copy-start.17 = (s32[64]{0:T(128)S(1)}, s32[64]{0:T(128)}, u32[]{:S(2)}) copy-start(s32[64]{0:T(128)} %param.19) | copy-start | bytes 772
  3.3 8.5 %copy-start.16 = (f32[512,28]{0,1:T(8,128)S(1)}, f32[512,28]{0,1:T(8,128)}, u32[]{:S(2)}) copy-start(f32[512,28]{0,1:T(8,128)} %param.14) | copy-start | bytes 172036
  3.3 35.1 %all-to-all-start = ((bf16[32,224,128]{2,1,0:T(8,128)(2,1)}), bf16[32,224,128]{2,1,0:T(8,128)(2,1)S(1)}, u32[]{:S(2)}, u32[]{:S(2)}) async-start(bf16[32,224,128]{2,1,0:T(8,128)(2,1)} %shard_map.116), calls=%async_computation | async-start | bytes 3670016 | tf_op jit(solution)/shard_map/all_to_all | solution.py:410
  10.7 1.4 copy-start.13
  11.4 7.0 %copy-start.7 = (s32[512,1]{1,0:T(8,128)}, s32[512,1]{1,0:T(8,128)S(1)}, u32[]{:S(2)}) copy-start(s32[512,1]{1,0:T(8,128)S(1)} %copy.21.start_ref) | copy-start | bytes 6148
  12.1 1.5 %copy-start.11 = (bf16[512,1792]{1,0:T(8,128)(2,1)S(1)}, bf16[512,1792]{1,0:T(8,128)(2,1)}, u32[]{:S(2)}) copy-start(bf16[512,1792]{1,0:T(8,128)(2,1)} %x_ref.3) | copy-start | bytes 5505028
  18.4 0.6 copy-start.9
  19.0 19.4 %collective-permute-start = (f32[56,1792]{1,0:T(8,128)S(1)}, f32[56,1792]{1,0:T(8,128)S(1)}, u32[]{:S(2)}, u32[]{:S(2)}) collective-permute-start(f32[56,1792]{1,0:T(8,128)S(1)} %get-tuple-element.21), channel_id=1, source_target_pairs={{0,4},{4,8},{8,12},{12,16},{16,20},{20,24},{24,28},{28,32},{32,36}... | collective-permute-start | bytes 1204232 | tf_op jit(solution)/shard_map/ppermute | solution.py:437
  21.2 1.5 %copy-start.5 = (bf16[128,7168]{1,0:T(8,128)(2,1)S(1)}, bf16[128,7168]{1,0:T(8,128)(2,1)}, u32[]{:S(2)}) copy-start(bf16[128,7168]{1,0:T(8,128)(2,1)} %refs_0_.2) | copy-start | bytes 5505028
  24.8 1.2 copy-start.3
  26.2 57.7 %copy-start.15 = (s32[4096]{0:T(1024)}, s32[4096]{0:T(1024)S(1)}, u32[]{:S(2)}) copy-start(s32[4096]{0:T(1024)S(1)} %broadcast_subtract_fusion) | copy-start | bytes 49156
  38.4 31.3 %all-to-all-start.2 = ((bf16[32,224,128]{2,1,0:T(8,128)(2,1)}), bf16[32,224,128]{2,1,0:T(8,128)(2,1)}, u32[]{:S(2)}, u32[]{:S(2)}) async-start(bf16[32,224,128]{2,1,0:T(8,128)(2,1)} %copy-done.3), calls=%async_computation.2 | async-start | bytes 3670016 | tf_op jit(solution)/shard_map/all_to_all | solution.py:410
  44.2 19.4 %collective-permute-start.1 = (bf16[12,224,128]{2,1,0:T(8,128)(2,1)S(1)}, bf16[12,224,128]{2,1,0:T(8,128)(2,1)S(1)}, u32[]{:S(2)}, u32[]{:S(2)}) collective-permute-start(bf16[12,224,128]{2,1,0:T(8,128)(2,1)S(1)} %slice.24), channel_id=1, source_target_pairs={{0,32},{32,64},{64,96},{1,33},{33,65},{65,97},{2,34},{34,66},{66,9... | collective-permute-start | bytes 2064392 | tf_op jit(solution)/shard_map/ppermute | solution.py:441
  47.7 21.0 %collective-permute-start.2 = (f32[16,1792]{1,0:T(8,128)}, f32[16,1792]{1,0:T(8,128)}, u32[]{:S(2)}, u32[]{:S(2)}) collective-permute-start(f32[16,1792]{1,0:T(8,128)} %copy-done.9), channel_id=1, source_target_pairs={{0,4},{4,8},{8,12},{12,16},{16,20},{20,24},{24,28},{28,32},{32,36}... | collective-permute-start | bytes 344072 | tf_op jit(solution)/shard_map/ppermute | solution.py:444
  49.6 1.5 %copy-start.6 = (bf16[128,7168]{1,0:T(8,128)(2,1)S(1)}, bf16[128,7168]{1,0:T(8,128)(2,1)}, u32[]{:S(2)}) copy-start(bf16[128,7168]{1,0:T(8,128)(2,1)} %refs_0_.3) | copy-start | bytes 5505028
  53.2 1.2 copy-start.2
  55.4 1.3 copy-start.1
  64.0 5.7 %copy-start.4 = (bf16[1536,224]{1,0:T(8,128)(2,1)}, bf16[1536,224]{1,0:T(8,128)(2,1)S(1)}, u32[]{:S(2)}) copy-start(bf16[1536,224]{1,0:T(8,128)(2,1)S(1)} %shard_map.118.halo_k) | copy-start | bytes 2064388
  69.7 30.3 %all-to-all-start.1 = ((bf16[32,224,128]{2,1,0:T(8,128)(2,1)}), bf16[32,224,128]{2,1,0:T(8,128)(2,1)}, u32[]{:S(2)}, u32[]{:S(2)}) async-start(bf16[32,224,128]{2,1,0:T(8,128)(2,1)} %copy-done.2), calls=%async_computation.1 | async-start | bytes 3670016 | tf_op jit(solution)/shard_map/all_to_all | solution.py:410
  74.5 4.8 %copy-start.10 = (f32[16,1792]{1,0:T(8,128)S(1)}, f32[16,1792]{1,0:T(8,128)}, u32[]{:S(2)}) copy-start(f32[16,1792]{1,0:T(8,128)} %copy-done.9) | copy-start | bytes 344068
  75.7 19.5 %collective-permute-start.3 = (bf16[12,224,128]{2,1,0:T(8,128)(2,1)S(1)}, bf16[12,224,128]{2,1,0:T(8,128)(2,1)}, u32[]{:S(2)}, u32[]{:S(2)}) collective-permute-start(bf16[12,224,128]{2,1,0:T(8,128)(2,1)S(1)} %slice.25), channel_id=1, source_target_pairs={{0,32},{32,64},{64,96},{1,33},{33,65},{65,97},{2,34},{34,66},{66,9... | collective-permute-start | bytes 2064392 | tf_op jit(solution)/shard_map/ppermute | solution.py:448
  80.2 33.9 %collective-permute-start.4 = (f32[64,1792]{1,0:T(8,128)S(1)}, f32[64,1792]{1,0:T(8,128)S(1)}, u32[]{:S(2)}, u32[]{:S(2)}) collective-permute-start(f32[64,1792]{1,0:T(8,128)S(1)} %maximum_add_fusion), channel_id=1, source_target_pairs={{0,8},{4,12},{8,16},{12,20},{16,24},{20,28},{24,32},{28,36},{32,40... | collective-permute-start | bytes 1376264 | tf_op jit(solution)/shard_map/ppermute | solution.py:455
  114.1 4.9 %copy-start.18 = (f32[28]{0:T(128)S(1)}, f32[28]{0:T(128)}, u32[]{:S(2)}) copy-start(f32[28]{0:T(128)} %param.18) | copy-start | bytes 340
  114.1 5.1 %copy-start.14 = (bf16[512,128]{1,0:T(8,128)(2,1)S(1)}, bf16[512,128]{1,0:T(8,128)(2,1)}, u32[]{:S(2)}) copy-start(bf16[512,128]{1,0:T(8,128)(2,1)} %param.16) | copy-start | bytes 393220
  114.1 5.2 %copy-start.8 = (s32[512,1]{1,0:T(8,128)S(1)}, s32[512,1]{1,0:T(8,128)}, u32[]{:S(2)}) copy-start(s32[512,1]{1,0:T(8,128)} %copy-done.7) | copy-start | bytes 6148
  114.1 30.5 %all-to-all-start.3 = ((bf16[32,224,128]{2,1,0:T(8,128)(2,1)}), bf16[32,224,128]{2,1,0:T(8,128)(2,1)}, u32[]{:S(2)}, u32[]{:S(2)}) async-start(bf16[32,224,128]{2,1,0:T(8,128)(2,1)} %shard_map.119), calls=%async_computation.3 | async-start | bytes 3670016 | tf_op jit(solution)/shard_map/all_to_all | solution.py:410
  119.3 1.5 %copy-start.12 = (bf16[512,1792]{1,0:T(8,128)(2,1)S(1)}, bf16[512,1792]{1,0:T(8,128)(2,1)}, u32[]{:S(2)}) copy-start(bf16[512,1792]{1,0:T(8,128)(2,1)} %x_ref.3) | copy-start | bytes 5505028
